TPU v7x, 32 devices: a whole 2x2x4 slice. The times are simulated.
32 devices in a mesh: seq: 16 (over z, y, core), exp: 2 (over x).
Axes of the slice: x: 2, y: 2, z: 4, core: 2. Of those that a mesh axis runs over, the one named last changes fastest.
Arguments:
- tokens: bfloat16 [2048, 2880], P('seq'), may hold values from -6 to 6
- expert_ids: int32 [2048, 4], P('seq'), may hold values from 0 to 15, all different within a row; in each aligned block of 128 rows (0 to 127, 128 to 255, ...) at most 48 rows name the same one
- route_weights: float32 [2048, 4], P('seq'), may hold values from 0.05 to 1
- cotangent: bfloat16 [2048, 2880], P('seq'), may hold values from -3 to 3
- w_gate: bfloat16 [16, 2880, 2048], P('seq', None, 'exp'), may hold values from -0.109375 to 0.109375
- w_up: bfloat16 [16, 2880, 2048], P('seq', None, 'exp'), may hold values from -0.109375 to 0.109375
- w_down: bfloat16 [16, 2048, 2880], P('seq', 'exp'), may hold values from -0.125 to 0.125
Outputs:
- moe_out: bfloat16 [2048, 2880], P('seq')
- token_grad: bfloat16 [2048, 2880], P('seq')
- weight_grad: float32 [2048, 4], P('seq')
- gate_proj_grad: bfloat16 [16, 2880, 2048], P('seq', None, 'exp')
- up_proj_grad: bfloat16 [16, 2880, 2048], P('seq', None, 'exp')
- down_proj_grad: bfloat16 [16, 2048, 2880], P('seq', 'exp')
Inputs may be any that keep to these rules, and one draw needn't show every extreme that they name: `expert_ids`: within the tokens of one slab (128 rows) no expert is named by more than 48 routes, a bound that some block reaches; the 4 ids of a row differ.
All inputs are finite; a program needn't handle non-finite values.
Results may differ from a plain program's by a relative error of at most 0.0058.
Values may be sent and summed in bfloat16 or wider, within the bound.
A program may use at most 256 MiB of HBM per device.

v0:
```python
import jax
import jax.numpy as jnp
from jax import lax
from jax.sharding import PartitionSpec as P


def dot_last(left, right):
    return lax.dot_general(
        left, right, (((1,), (1,)), ((), ())), preferred_element_type=jnp.float32
    )


def dot_first(left, right):
    return lax.dot_general(
        left, right, (((0,), (0,)), ((), ())), preferred_element_type=jnp.float32
    )


def route_slots(expert_ids, experts, capacity):
    flat = expert_ids.reshape(-1)
    onehot = (flat[:, None] == jnp.arange(experts, dtype=jnp.int32)[None, :]).astype(jnp.int32)
    slot = jnp.sum((jnp.cumsum(onehot, axis=0) - 1) * onehot, axis=1)
    return (flat * capacity + slot, jnp.sum(onehot, axis=0))


def expert_rows(x_rows, r_rows, w_gate, w_up, w_down):
    gate = jnp.dot(x_rows, w_gate, preferred_element_type=jnp.float32)
    up = jnp.dot(x_rows, w_up, preferred_element_type=jnp.float32)
    sigma = jax.nn.sigmoid(gate)
    silu = gate * sigma
    hidden = (silu * up).astype(jnp.bfloat16)
    y_part = jnp.dot(hidden, w_down, preferred_element_type=jnp.float32)
    d_hidden = dot_last(r_rows, w_down)
    d_gate = (d_hidden * up * sigma * (1.0 + gate * (1.0 - sigma))).astype(jnp.bfloat16)
    d_up = (d_hidden * silu).astype(jnp.bfloat16)
    dx_part = dot_last(d_gate, w_gate) + dot_last(d_up, w_up)
    sums = (dot_first(x_rows, d_gate), dot_first(x_rows, d_up), dot_first(hidden, r_rows))
    return (y_part, dx_part, sums)


def body(tokens, expert_ids, route_weights, cotangent, w_gate, w_up, w_down):
    tok, width = tokens.shape
    top = expert_ids.shape[1]
    experts = lax.axis_size("seq")
    capacity = 3 * tok * top // (2 * experts)
    total = experts * capacity
    target, counts = route_slots(expert_ids, experts, capacity)
    x_routes = jnp.repeat(tokens, top, axis=0)
    scaled = (
        (route_weights[:, :, None] * cotangent[:, None, :].astype(jnp.float32))
        .astype(jnp.bfloat16)
        .reshape(tok * top, width)
    )
    x_send = (
        jnp.zeros((total, width), jnp.bfloat16)
        .at[target]
        .set(x_routes)
        .reshape(experts, capacity, width)
    )
    r_send = (
        jnp.zeros((total, width), jnp.bfloat16)
        .at[target]
        .set(scaled)
        .reshape(experts, capacity, width)
    )
    x_recv, r_recv = (
        lax.all_to_all(x_send, "seq", split_axis=0, concat_axis=0, tiled=True),
        lax.all_to_all(r_send, "seq", split_axis=0, concat_axis=0, tiled=True),
    )
    x_recv = x_recv.reshape(total, width)
    r_recv = r_recv.reshape(total, width)
    gate_weight = w_gate[0]
    up_weight = w_up[0]
    down_weight = w_down[0]
    y_part, dx_part, sums = expert_rows(x_recv, r_recv, gate_weight, up_weight, down_weight)
    upstream = cotangent.astype(jnp.float32)
    y_back, dx_back = (
        lax.all_to_all(
            y_part.reshape(experts, capacity, width), "seq", split_axis=0, concat_axis=0, tiled=True
        ),
        lax.all_to_all(
            dx_part.reshape(experts, capacity, width),
            "seq",
            split_axis=0,
            concat_axis=0,
            tiled=True,
        ),
    )
    y_routes = y_back.reshape(total, width)[target].reshape(tok, top, width)
    dx_routes = dx_back.reshape(total, width)[target].reshape(tok, top, width)
    y_sum = jnp.sum(route_weights[:, :, None] * y_routes, axis=1)
    dx_sum = jnp.sum(dx_routes, axis=1)
    products = jnp.sum(y_routes * upstream[:, None, :], axis=2)
    y_full, dx_full, weight_grad = lax.psum((y_sum, dx_sum, products), "exp")
    return (
        y_full.astype(jnp.bfloat16),
        dx_full.astype(jnp.bfloat16),
        weight_grad,
        sums[0].astype(jnp.bfloat16)[None],
        sums[1].astype(jnp.bfloat16)[None],
        sums[2].astype(jnp.bfloat16)[None],
    )


def solution(mesh):
    placed = (
        P("seq", None),
        P("seq", None),
        P("seq", None),
        P("seq", None),
        P("seq", None, "exp"),
        P("seq", None, "exp"),
        P("seq", "exp", None),
    )
    return jax.shard_map(
        body,
        mesh=mesh,
        in_specs=placed,
        out_specs=(
            P("seq", None),
            P("seq", None),
            P("seq", None),
            P("seq", None, "exp"),
            P("seq", None, "exp"),
            P("seq", "exp", None),
        ),
        check_vma=False,
    )
```

profile of v0, /device:TPU:12, one launch (start us, length us, event | category | flops | bytes accessed | tf_op | source)
XLA Modules:
  0.0 774.8 jit_solution(5180759045507434284)
XLA Ops:
  0.6 0.7 broadcast_multiply_fusion
  1.3 0.8 copy.28
  2.1 0.1 eq.25
  2.2 0.1 eq.29
  2.3 0.1 copy.27
  2.4 0.1 mul.79
  2.6 1.2 reduce-window.6
  3.7 0.2 slice_reduce_fusion
  4.0 1.4 copy.33
  5.4 3.6 mul.86
  9.0 0.0 copy-start.1
  9.0 7.8 %mul.87 = f32[512,2880]{1,0:T(8,128)} reshape(f32[128,4,2880]{2,1,0:T(4,128)} %mul.86) | data formatting | bytes 11796480 | tf_op jit(solution)/shard_map/mul | solution.py:50
  16.7 0.0 copy-done.1
  16.7 0.1 copy.26
  16.9 0.1 mul.84
  17.0 0.1 fusion.22
  17.1 9.7 %scatter_custom_fusion.1 = bf16[768,2880]{1,0:T(8,128)(2,1)} fusion(s32[512]{0:T(512)S(1)} %bitcast.66, f32[512,2880]{1,0:T(8,128)} %mul.87, f32[512]{0:T(512)S(1)} %mul.84, bf16[]{:T(256)} %constant.7.clone.1), kind=kCustom, calls=%fused_computation.28 | custom fusion | flops 2949120 | bytes 10323970 | tf_op jit(solution)/shard_map/scatter | solution.py:63
  26.8 0.0 copy-start
  26.8 7.0 all-to-all-start.2
  33.8 0.0 copy-done
  33.8 0.3 copy.31
  34.1 2.4 broadcast_in_dim.8
  36.5 5.6 reshape.140
  42.1 8.8 %scatter_custom_fusion = bf16[768,2880]{1,0:T(8,128)(2,1)} fusion(s32[512]{0:T(512)S(1)} %bitcast.67, bf16[512,2880]{1,0:T(8,128)(2,1)} %reshape.140, bf16[]{:T(256)} %constant.7.clone.1), kind=kCustom, calls=%fused_computation.31 | custom fusion | bytes 4424192 | tf_op jit(solution)/shard_map/scatter | solution.py:57
  50.9 82.0 %all-to-all-done.2 = bf16[16,48,2880]{2,1,0:T(8,128)(2,1)} async-done(((bf16[16,48,2880]{2,1,0:T(8,128)(2,1)}), bf16[16,48,2880]{2,1,0:T(8,128)(2,1)}, u32[]{:S(2)}, u32[]{:S(2)}) %all-to-all-start.2) | async-done | bytes 4423712 | tf_op jit(solution)/shard_map/all_to_all | solution.py:68
  133.0 5.3 all-to-all-start
  138.3 9.5 %fusion.2 = f32[768,1024]{1,0:T(8,128)} fusion(bf16[768,2880]{1,0:T(8,128)(2,1)} %bitcast.12, bf16[1,1024,2880]{1,2,0:T(8,128)(2,1)} %param.13), kind=kOutput, calls=%fused_computation.9 | convolution fusion | flops 4529848320 | bytes 13467648 | tf_op jit(solution)/shard_map/dot_general | solution.py:8
  147.9 89.7 %all-to-all-done = bf16[16,48,2880]{2,1,0:T(8,128)(2,1)} async-done(((bf16[16,48,2880]{2,1,0:T(8,128)(2,1)}), bf16[16,48,2880]{2,1,0:T(8,128)(2,1)}, u32[]{:S(2)}, u32[]{:S(2)}) %all-to-all-start) | async-done | bytes 4423712 | tf_op jit(solution)/shard_map/all_to_all | solution.py:67
  237.5 0.0 copy-start.5
  237.5 0.0 slice-start
  237.5 8.5 %fusion.6 = f32[768,1024]{1,0:T(8,128)S(1)} fusion(bf16[768,2880]{1,0:T(8,128)(2,1)} %bitcast.4, bf16[1,2880,1024]{2,1,0:T(8,128)(2,1)} %param.12), kind=kOutput, calls=%fused_computation.13 | convolution fusion | flops 4529848320 | bytes 13467648 | tf_op jit(solution)/shard_map/dot_general | solution.py:28
  246.1 0.0 copy-done.5
  246.1 0.0 slice-start.1
  246.1 11.1 %multiply_convert_fusion.2 = (bf16[768,1024]{1,0:T(8,128)(2,1)}, bf16[768,1024]{1,0:T(8,128)(2,1)}, bf16[768,1024]{1,0:T(8,128)(2,1)S(1)}) fusion(f32[768,1024]{1,0:T(8,128)S(1)} %copy-done.5, f32[768,1024]{1,0:T(8,128)S(1)} %fusion.6, bf16[768,2880]{1,0:T(8,128)(2,1)} %bitcast.4, bf16[1,2880,1024]{2,1,0:T(8,128)(2,1)} %param.11), kind=kOutput, calls=%fused_computation.24 | convolution fusion | flops 4541644800 | bytes 21331968 | tf_op jit(solution)/shard_map/dot_general | solution.py:27
  257.2 0.0 copy-start.2
  257.2 1.1 copy-done.2
  258.3 0.0 slice-done
  258.3 0.0 slice-done.1
  258.3 7.4 fusion
  265.7 5.0 all-to-all-start.1
  270.7 7.5 fusion.4
  278.3 0.0 copy-done.4
  278.3 9.8 %fusion.12 = f32[768,2880]{0,1:T(8,128)} fusion(f32[768,2880]{0,1:T(8,128)S(1)} %fusion.4, bf16[768,1024]{1,0:T(8,128)(2,1)S(1)} %copy-done.4, bf16[1,2880,1024]{2,1,0:T(8,128)(2,1)} %param.11), kind=kOutput, calls=%fused_computation.22 | convolution fusion | flops 4532060160 | bytes 25165824 | tf_op jit(solution)/shard_map/dot_general | solution.py:8
  288.1 9.4 %copy.34 = f32[768,2880]{1,0:T(8,128)} copy(f32[768,2880]{0,1:T(8,128)} %fusion.12) | data formatting | bytes 17694720 | tf_op jit(solution)/shard_map/add | solution.py:36
  297.5 169.5 %all-to-all-done.1 = f32[16,48,2880]{2,1,0:T(8,128)} async-done(((f32[16,48,2880]{2,1,0:T(8,128)}), f32[16,48,2880]{2,1,0:T(8,128)}, u32[]{:S(2)}, u32[]{:S(2)}) %all-to-all-start.1) | async-done | bytes 8847392 | tf_op jit(solution)/shard_map/all_to_all | solution.py:78
  467.0 5.4 all-to-all-start.3
  472.4 0.0 copy-start.6
  472.4 10.3 %convert_bitcast_fusion.2 = bf16[1,2880,1024]{2,1,0:T(8,128)(2,1)} fusion(bf16[768,2880]{1,0:T(8,128)(2,1)} %bitcast.4, bf16[768,1024]{1,0:T(8,128)(2,1)} %get-tuple-element.17), kind=kOutput, calls=%fused_computation.21 | convolution fusion | flops 4532797440 | bytes 11894784 | tf_op jit(solution)/shard_map/dot_general | solution.py:14
  482.7 0.0 copy-done.6
  482.7 0.0 copy-start.3
  482.7 9.0 %convert_bitcast_fusion.1 = bf16[1,2880,1024]{2,1,0:T(8,128)(2,1)} fusion(bf16[768,2880]{1,0:T(8,128)(2,1)} %bitcast.4, bf16[768,1024]{1,0:T(8,128)(2,1)S(1)} %copy-done.6), kind=kOutput, calls=%fused_computation.20 | convolution fusion | flops 4532797440 | bytes 11894784 | tf_op jit(solution)/shard_map/dot_general | solution.py:14
  491.7 0.0 copy-done.3
  491.7 8.9 %convert_bitcast_fusion = bf16[1,1024,2880]{1,2,0:T(8,128)(2,1)} fusion(bf16[768,1024]{1,0:T(8,128)(2,1)S(1)} %copy-done.3, bf16[768,2880]{1,0:T(8,128)(2,1)} %bitcast.12), kind=kOutput, calls=%fused_computation.19 | convolution fusion | flops 4532797440 | bytes 11894784 | tf_op jit(solution)/shard_map/dot_general | solution.py:14
  500.6 10.5 %gather_fusion = f32[512,2880]{1,0:T(8,128)} fusion(f32[768,2880]{1,0:T(8,128)} %bitcast.10, s32[1024]{0:T(1024)S(1)} %pad_clamp_fusion), kind=kCustom, calls=%fused_computation | custom fusion | bytes 11798528 | tf_op jit(solution)/shard_map/gather | solution.py:89
  511.1 7.9 %reshape.114 = f32[128,4,2880]{2,1,0:T(4,128)} reshape(f32[512,2880]{1,0:T(8,128)} %gather_fusion) | data formatting | bytes 11796480 | tf_op jit(solution)/shard_map/reshape | solution.py:89
  519.0 13.9 %multiply_reduce_fusion = (f32[128,4]{1,0:T(8,128)S(1)}, f32[128,2880]{1,0:T(8,128)S(1)}) fusion(f32[128,4,2880]{2,1,0:T(4,128)} %reshape.114, f32[128,2880]{1,0:T(8,128)S(1)} %copy.33, f32[128,4]{1,0:T(8,128)S(1)} %copy.26), kind=kLoop, calls=%fused_computation.4 | loop fusion | flops 5529088 | bytes 8851456 | tf_op jit(solution)/shard_map/reduce_sum | solution.py:93
  532.9 135.6 %all-to-all-done.3 = f32[16,48,2880]{2,1,0:T(8,128)} async-done(((f32[16,48,2880]{2,1,0:T(8,128)}), f32[16,48,2880]{2,1,0:T(8,128)}, u32[]{:S(2)}, u32[]{:S(2)}) %all-to-all-start.3) | async-done | bytes 8847392 | tf_op jit(solution)/shard_map/all_to_all | solution.py:81
  668.5 10.6 %gather_fusion.1 = f32[512,2880]{1,0:T(8,128)} fusion(f32[768,2880]{1,0:T(8,128)} %bitcast.14, s32[1024]{0:T(1024)S(1)} %pad_clamp_fusion), kind=kCustom, calls=%fused_computation.1 | custom fusion | bytes 11798528 | tf_op jit(solution)/shard_map/gather | solution.py:90
  679.1 7.6 reshape.119
  686.7 6.3 reduce_sum.41
  693.0 76.2 %all-reduce.2 = (bf16[128,2880]{1,0:T(8,128)(2,1)}, bf16[128,2880]{1,0:T(8,128)(2,1)}, f32[128,4]{1,0:T(8,128)S(1)}) all-reduce(f32[128,2880]{1,0:T(8,128)S(1)} %get-tuple-element.13, f32[128,2880]{1,0:T(8,128)S(1)} %reduce_sum.41, f32[128,4]{1,0:T(8,128)S(1)} %get-tuple-element.12), channel_id=1, replica_groups=mesh['seq'=16,'exp'=2] {'exp'}, use_global_device_ids=true, to_apply=%region_5.6 | all-reduce | flops 737792 | bytes 4427776 | tf_op jit(solution)/shard_map/psum | solution.py:94
  769.2 2.3 copy.35
  771.4 2.3 copy.36
  773.7 0.7 copy.37
  (7 shorter events, 0.1 us)
Async XLA Ops:
  9.0 7.8 %copy-start.1 = (f32[128,4]{0,1:T(4,128)S(1)}, f32[128,4]{0,1:T(4,128)}, u32[]{:S(2)}) copy-start(f32[128,4]{0,1:T(4,128)} %param.9) | copy-start | bytes 6148
  26.8 7.0 copy-start
  26.8 106.2 %all-to-all-start.2 = ((bf16[16,48,2880]{2,1,0:T(8,128)(2,1)}), bf16[16,48,2880]{2,1,0:T(8,128)(2,1)}, u32[]{:S(2)}, u32[]{:S(2)}) async-start(bf16[16,48,2880]{2,1,0:T(8,128)(2,1)} %bitcast.64), calls=%async_computation.2 | async-start | bytes 9043968 | tf_op jit(solution)/shard_map/all_to_all | solution.py:68
  133.0 104.6 %all-to-all-start = ((bf16[16,48,2880]{2,1,0:T(8,128)(2,1)}), bf16[16,48,2880]{2,1,0:T(8,128)(2,1)}, u32[]{:S(2)}, u32[]{:S(2)}) async-start(bf16[16,48,2880]{2,1,0:T(8,128)(2,1)} %bitcast.65), calls=%async_computation | async-start | bytes 9043968 | tf_op jit(solution)/shard_map/all_to_all | solution.py:67
  237.5 8.6 %copy-start.5 = (f32[768,1024]{1,0:T(8,128)S(1)}, f32[768,1024]{1,0:T(8,128)}, u32[]{:S(2)}) copy-start(f32[768,1024]{1,0:T(8,128)} %fusion.2) | copy-start | bytes 9437188
  237.5 20.8 %slice-start = ((s8[5898240]{0:T(1024)(128)(4,1)}), s8[4194304]{0:T(1024)(128)(4,1)S(1)}, s32[]{:S(2)}) async-start(s8[5898240]{0:T(1024)(128)(4,1)} %bitcast.70), calls=%async_computation.4 | async-start | bytes 8388608
  246.1 12.3 %slice-start.1 = ((s8[5898240]{0:T(1024)(128)(4,1)}), s8[1703936]{0:T(1024)(128)(4,1)S(1)}, s32[]{:S(2)}) async-start(s8[5898240]{0:T(1024)(128)(4,1)} %bitcast.70), calls=%async_computation.5 | async-start | bytes 3407872
  257.2 1.2 copy-start.2
  265.7 201.3 %all-to-all-start.1 = ((f32[16,48,2880]{2,1,0:T(8,128)}), f32[16,48,2880]{2,1,0:T(8,128)}, u32[]{:S(2)}, u32[]{:S(2)}) async-start(f32[16,48,2880]{2,1,0:T(8,128)} %fusion), calls=%async_computation.1 | async-start | bytes 18087936 | tf_op jit(solution)/shard_map/all_to_all | solution.py:78
  270.7 7.6 copy-start.4
  467.0 201.5 %all-to-all-start.3 = ((f32[16,48,2880]{2,1,0:T(8,128)}), f32[16,48,2880]{2,1,0:T(8,128)}, u32[]{:S(2)}, u32[]{:S(2)}) async-start(f32[16,48,2880]{2,1,0:T(8,128)} %bitcast.63), calls=%async_computation.3 | async-start | bytes 18087936 | tf_op jit(solution)/shard_map/all_to_all | solution.py:81
  472.4 10.3 %copy-start.6 = (bf16[768,1024]{1,0:T(8,128)(2,1)S(1)}, bf16[768,1024]{1,0:T(8,128)(2,1)}, u32[]{:S(2)}) copy-start(bf16[768,1024]{1,0:T(8,128)(2,1)} %get-tuple-element.18) | copy-start | bytes 4718596
  482.7 9.0 %copy-start.3 = (bf16[768,1024]{1,0:T(8,128)(2,1)S(1)}, bf16[768,1024]{1,0:T(8,128)(2,1)}, u32[]{:S(2)}) copy-start(bf16[768,1024]{1,0:T(8,128)(2,1)} %copy-done.2) | copy-start | bytes 4718596
where the time goes:
time: 783 us; the launch traced here: 775 us
  waiting for transfers between devices  477 us (61%)
  local copies, waits for them, and re-layouts  83.9 us (11%)
  matrix products  82 us (10%)
  blocking collectives  76.2 us (10%)
  other arithmetic  31.9 us (4%)
  starting transfers between devices  22.8 us (3%)
    all_to_all x1, waiting for transfers between devices, body(): lax.all_to_all(y_part.reshape(experts, capacity, width), 'seq', split_axi...  169 us
    all_to_all x1, waiting for transfers between devices, body(): lax.all_to_all(dx_part.reshape(experts, capacity, width), 'seq', split_ax...  136 us
    all_to_all x1, waiting for transfers between devices, body(): lax.all_to_all(x_send, 'seq', split_axis=0, concat_axis=0, tiled=True)  89.7 us
    all_to_all x1, waiting for transfers between devices, body(): lax.all_to_all(r_send, 'seq', split_axis=0, concat_axis=0, tiled=True)  82 us
    psum x1, blocking collectives, body(): y_full, dx_full, weight_grad = lax.psum((y_sum, dx_sum, products), 'exp')  76.2 us
    dot_general x3, matrix products, dot_first(): lax.dot_general(left, right, (((0,), (0,)), ((), ())), preferred_element_...  28.2 us
    dot_general x3, matrix products, dot_last(): lax.dot_general(left, right, (((1,), (1,)), ((), ())), preferred_element_...  26.9 us
  transfers between devices with their start and end apart: 4, of which 4 were waited for; matrix products, arithmetic and copies ran while one was open for 15% of the time, Pallas kernels for 0%

commit v1 on v0

v1 whole, which is shorter than its diff:
```python
import jax
import jax.numpy as jnp
from jax import lax
from jax.sharding import PartitionSpec as P


def dot(left, right, dims):
    return lax.dot_general(left, right, (dims, ((), ())), preferred_element_type=jnp.float32)


def body(tokens, expert_ids, route_weights, cotangent, w_gate, w_up, w_down):
    tok, width = tokens.shape
    top = expert_ids.shape[1]
    experts = lax.axis_size("seq")
    shares = lax.axis_size("exp")
    rows = 3 * tok * top // 2
    share = tok // shares
    me = lax.axis_index("seq")
    mine = lax.axis_index("exp")
    both = ("seq", "exp")
    meta = jnp.concatenate([expert_ids.astype(jnp.float32), route_weights], axis=1)
    meta = lax.all_gather(meta, "seq", axis=0, tiled=True)
    x_all = lax.all_gather(
        lax.dynamic_slice_in_dim(tokens, mine * share, share, 0), both, axis=0, tiled=True
    )
    c_all = lax.all_gather(
        lax.dynamic_slice_in_dim(cotangent, mine * share, share, 0), both, axis=0, tiled=True
    )
    match = meta[:, :top] == me.astype(jnp.float32)
    g_tok = jnp.sum(jnp.where(match, meta[:, top:], 0.0), axis=1)
    hit = jnp.any(match, axis=1)
    slabs = hit.reshape(experts, tok)
    before = (jnp.arange(tok)[:, None] < jnp.arange(tok)[None, :]).astype(jnp.bfloat16)
    within = dot(slabs.astype(jnp.bfloat16), before, ((1,), (0,))).astype(jnp.int32)
    counts = jnp.sum(slabs.astype(jnp.int32), axis=1)
    earlier = jnp.arange(experts)[None, :] < jnp.arange(experts)[:, None]
    starts = jnp.sum(jnp.where(earlier, counts[None, :], 0), axis=1)
    place = jnp.where(slabs, within + starts[:, None], -1).reshape(-1)
    pick = jnp.arange(rows, dtype=jnp.int32)[:, None] == place[None, :]
    spread = (place[:, None] == jnp.arange(rows, dtype=jnp.int32)[None, :]).astype(jnp.bfloat16)
    g_row = jnp.sum(jnp.where(pick, g_tok[None, :], 0.0), axis=1)[:, None]
    pick_b = pick.astype(jnp.bfloat16)
    wg, wu, wd = w_gate[0], w_up[0], w_down[0]

    x_rows = dot(pick_b, x_all, ((1,), (0,))).astype(jnp.bfloat16)
    gate = dot(x_rows, wg, ((1,), (0,)))
    up = dot(x_rows, wu, ((1,), (0,)))
    sigma = jax.nn.sigmoid(gate)
    silu = gate * sigma
    hidden = silu * up
    hidden_g = (hidden * g_row).astype(jnp.bfloat16)
    y_rows = dot(hidden_g, wd, ((1,), (0,))).astype(jnp.bfloat16)
    y_all = dot(spread, y_rows, ((1,), (0,))).astype(jnp.bfloat16)
    moe = lax.psum_scatter(y_all, both, scatter_dimension=0, tiled=True)

    c_rows = dot(pick_b, c_all, ((1,), (0,))).astype(jnp.bfloat16)
    d_cot = dot(c_rows, wd, ((1,), (1,)))
    d_hidden = d_cot * g_row
    d_gate = (d_hidden * up * sigma * (1.0 + gate * (1.0 - sigma))).astype(jnp.bfloat16)
    d_up = (d_hidden * silu).astype(jnp.bfloat16)
    wgt = jnp.sum(hidden * d_cot, axis=1)
    dx_rows = (dot(d_gate, wg, ((1,), (1,))) + dot(d_up, wu, ((1,), (1,)))).astype(jnp.bfloat16)
    dx_all = dot(spread, dx_rows, ((1,), (0,))).astype(jnp.bfloat16)
    dx = lax.psum_scatter(dx_all, both, scatter_dimension=0, tiled=True)

    wgt_tok = jnp.sum(jnp.where(pick, wgt[:, None], 0.0), axis=0).reshape(experts, tok)
    wgt_back = lax.all_to_all(wgt_tok, "seq", split_axis=0, concat_axis=0, tiled=True)
    named = expert_ids[:, :, None] == jnp.arange(experts, dtype=jnp.int32)[None, None, :]
    weight_grad = jnp.sum(jnp.where(named, wgt_back.T[:, None, :], 0.0), axis=2)
    weight_grad = lax.psum(weight_grad, "exp")

    g_gate = dot(x_rows, d_gate, ((0,), (0,))).astype(jnp.bfloat16)
    g_up = dot(x_rows, d_up, ((0,), (0,))).astype(jnp.bfloat16)
    g_down = dot(hidden_g, c_rows, ((0,), (0,))).astype(jnp.bfloat16)
    moe, dx = lax.all_gather((moe, dx), "exp", axis=0, tiled=True)
    return moe, dx, weight_grad, g_gate[None], g_up[None], g_down[None]


def solution(mesh):
    rows = P("seq", None)
    columns = P("seq", None, "exp")
    down = P("seq", "exp", None)
    return jax.shard_map(
        body,
        mesh=mesh,
        in_specs=(rows, rows, rows, rows, columns, columns, down),
        out_specs=(rows, rows, rows, columns, columns, down),
        check_vma=False,
    )
```

time: 783 us -> 813 us (1.038)
  waiting for transfers between devices: 477 us -> 595 us
  local copies, waits for them, and re-layouts: 83.9 us -> 8.4 us
  matrix products: 82 us -> 130 us
  blocking collectives: 76.2 us -> 42.8 us
  other arithmetic: 31.9 us -> 6.17 us
  starting transfers between devices: 22.8 us -> 5.33 us
  between operations: 1.23 us -> 14.5 us
    all_to_all x4 -> x1, waiting for transfers between devices: 477 us -> 0.01 us  [body(): lax.all_to_all(wgt_tok, 'seq', split_axis=0, concat_axis=0, tiled=True)]
    reduce_scatter x0 -> x2, waiting for transfers between devices: none -> 452 us  [the longest x1 251 us: body(): moe = lax.psum_scatter(y_all, both, scatter_dimension=0, tiled=True)]
    all_gather x0 -> x2, waiting for transfers between devices: none -> 143 us  [the longest x1 78 us: body(): lax.all_gather(lax.dynamic_slice_in_dim(tokens, mine * share, share, 0),...]
    psum x1, blocking collectives: 76.2 us -> 5.97 us  [body(): weight_grad = lax.psum(weight_grad, 'exp')]
    dot_general x9 -> x14, matrix products: 82 us -> 130 us  [dot(): lax.dot_general(left, right, (dims, ((), ())), preferred_element_type=jnp...]
    all_gather x0 -> x3, blocking collectives: none -> 36.9 us  [the longest x2 21.5 us: body(): moe, dx = lax.all_gather((moe, dx), 'exp', axis=0, tiled=True)]
    reshape x3 -> x0, local copies, waits for them, and re-layouts: 21.1 us -> none  [the longest x1 7.88 us: body(): y_routes = y_back.reshape(total, width)[target].reshape(tok, top, width)]
    gather x2 -> x0, local copies, waits for them, and re-layouts: 21.1 us -> none  [the longest x1 10.6 us: body(): dx_routes = dx_back.reshape(total, width)[target].reshape(tok, top, width)]
  transfers between devices with their start and end apart: 4 -> 5, of which waited for: 4 -> 4; matrix products, arithmetic and copies ran while one was open for 15% -> 10% of each run, Pallas kernels for 0% -> 0%
where the time goes in v1:
time: 813 us; the launch traced here: 802 us
  waiting for transfers between devices  595 us (73%)
  matrix products  130 us (16%)
  blocking collectives  42.8 us (5%)
  between operations  14.5 us (2%)
  local copies, waits for them, and re-layouts  8.4 us (1%)
    reduce_scatter x1, waiting for transfers between devices, body(): moe = lax.psum_scatter(y_all, both, scatter_dimension=0, tiled=True)  251 us
    reduce_scatter x1, waiting for transfers between devices, body(): dx = lax.psum_scatter(dx_all, both, scatter_dimension=0, tiled=True)  201 us
    dot_general x14, matrix products, dot(): lax.dot_general(left, right, (dims, ((), ())), preferred_element_type=jnp...  130 us
    all_gather x1, waiting for transfers between devices, body(): lax.all_gather(lax.dynamic_slice_in_dim(tokens, mine * share, share, 0),...  78 us
    all_gather x1, waiting for transfers between devices, body(): lax.all_gather(lax.dynamic_slice_in_dim(cotangent, mine * share, share, 0...  65.2 us
    all_gather x2, blocking collectives, body(): moe, dx = lax.all_gather((moe, dx), 'exp', axis=0, tiled=True)  21.5 us
  transfers between devices with their start and end apart: 5, of which 4 were waited for; matrix products, arithmetic and copies ran while one was open for 10% of the time, Pallas kernels for 0%

profile of v1, /device:TPU:12, one launch (start us, length us, event | category | flops | bytes accessed | tf_op | source)
XLA Modules:
  0.0 802.4 jit_solution(14544434809815293873)
XLA Ops:
  7.2 0.0 copy-start
  7.2 0.0 copy-start.8
  7.2 0.0 copy-start.10
  7.2 0.0 all-gather.3.cloned.1.call-start
  7.3 1.0 copy-done
  8.3 0.3 constant_dynamic-slice_fusion
  8.6 1.0 copy.32
  9.6 0.0 all-gather.3.cloned.1.call-update
  9.6 0.0 all-gather.5.cloned.1.call-start
  9.6 1.4 constant_dynamic-slice_fusion.1
  11.0 1.0 copy.33
  12.0 0.0 all-gather.5.cloned.1.call-update
  12.1 0.0 reduce-scatter.5.cloned.1.call-start
  12.1 0.0 copy-done.8
  12.1 0.0 copy-done.10
  12.2 15.4 %all_gather.15 = f32[2048,8]{0,1:T(8,128)S(1)} all-gather(f32[128,8]{0,1:T(8,128)S(1)} %pad_maximum_fusion), channel_id=1, replica_groups=mesh['seq'=16,'exp'=2] {'seq'}, dimensions={0}, use_global_device_ids=true | all-gather | bytes 69632 | tf_op jit(solution)/shard_map/all_gather | solution.py:22
  27.6 0.1 convert_reduce_fusion
  27.7 0.1 select_reduce_fusion.3
  27.9 0.1 fusion.30
  28.0 78.0 %all-gather.3.cloned.1.call-done = bf16[2048,2880]{1,0:T(8,128)(2,1)} async-done(((bf16[64,2880]{1,0:T(8,128)(2,1)}), bf16[2048,2880]{1,0:T(8,128)(2,1)}) %all-gather.3.cloned.1.call-update) | async-done | bytes 11796496 | tf_op jit(solution)/shard_map/all_gather | solution.py:23
  105.9 13.3 %fusion.17 = bf16[768,2880]{0,1:T(8,128)(2,1)S(1)} fusion(bf16[2048,2880]{1,0:T(8,128)(2,1)} %all-gather.3.cloned.1.call-done, s32[2048]{0:T(1024)S(1)} %fusion.30), kind=kOutput, calls=%fused_computation.25 | convolution fusion | flops 9063481344 | bytes 16228352 | tf_op jit(solution)/shard_map/dot_general | solution.py:8
  119.2 0.0 copy-start.11
  119.3 8.7 %fusion.12 = f32[768,1024]{1,0:T(8,128)S(1)} fusion(bf16[768,2880]{0,1:T(8,128)(2,1)S(1)} %fusion.17, bf16[1,2880,1024]{2,1,0:T(8,128)(2,1)} %param.11), kind=kOutput, calls=%fused_computation.19 | convolution fusion | flops 4529848320 | bytes 13467648 | tf_op jit(solution)/shard_map/dot_general | solution.py:8
  128.0 0.0 copy-done.11
  128.0 8.2 %fusion.8 = f32[768,1024]{1,0:T(8,128)} fusion(bf16[768,2880]{0,1:T(8,128)(2,1)S(1)} %fusion.17, bf16[1,2880,1024]{2,1,0:T(8,128)(2,1)} %param.12), kind=kOutput, calls=%fused_computation.15 | convolution fusion | flops 4529848320 | bytes 13467648 | tf_op jit(solution)/shard_map/dot_general | solution.py:8
  136.3 65.2 %all-gather.5.cloned.1.call-done = bf16[2048,2880]{1,0:T(8,128)(2,1)} async-done(((bf16[64,2880]{1,0:T(8,128)(2,1)}), bf16[2048,2880]{1,0:T(8,128)(2,1)}) %all-gather.5.cloned.1.call-update) | async-done | bytes 11796496 | tf_op jit(solution)/shard_map/all_gather | solution.py:26
  201.4 13.6 %fusion.18 = bf16[768,2880]{0,1:T(8,128)(2,1)S(1)} fusion(bf16[2048,2880]{1,0:T(8,128)(2,1)} %all-gather.5.cloned.1.call-done, s32[2048]{0:T(1024)S(1)} %fusion.30), kind=kOutput, calls=%fused_computation.26 | convolution fusion | flops 9063481344 | bytes 16228352 | tf_op jit(solution)/shard_map/dot_general | solution.py:8
  215.0 0.0 copy-done.2
  215.1 0.0 copy-start.12
  215.1 9.3 %multiply_reduce_fusion = (f32[768]{0:T(1024)S(1)}, f32[768,1024]{1,0:T(8,128)S(1)}) fusion(f32[768,1024]{1,0:T(8,128)S(1)} %copy-done.2, f32[768,1024]{1,0:T(8,128)S(1)} %fusion.12, bf16[768,2880]{0,1:T(8,128)(2,1)S(1)} %fusion.18, bf16[1,1024,2880]{1,2,0:T(8,128)(2,1)} %param.13), kind=kOutput, calls=%fused_computation.27 | convolution fusion | flops 4535352320 | bytes 19762176 | tf_op jit(solution)/shard_map/dot_general | solution.py:8
  224.4 0.0 copy-done.12
  224.4 2.3 select_reduce_fusion
  226.7 3.5 multiply_convert_fusion.1
  230.3 11.2 %fusion.6 = f32[768,2880]{0,1:T(8,128)} fusion(bf16[768,1024]{1,0:T(8,128)(2,1)S(1)} %get-tuple-element.35, bf16[1,2880,1024]{2,1,0:T(8,128)(2,1)} %param.12), kind=kOutput, calls=%fused_computation.13 | convolution fusion | flops 4529848320 | bytes 16318464 | tf_op jit(solution)/shard_map/dot_general | solution.py:8
  241.4 0.0 copy-done.5
  241.4 0.0 copy-done.3
  241.4 0.0 slice-done
  241.4 0.0 slice-done.1
  241.5 7.4 add_convert_fusion
  248.8 12.8 %convolution_convert_fusion = bf16[2048,2880]{1,0:T(8,128)(2,1)} fusion(bf16[768,2880]{0,1:T(8,128)(2,1)S(1)} %add_convert_fusion, s32[2048]{0:T(1024)S(1)} %fusion.30), kind=kOutput, calls=%fused_computation | convolution fusion | flops 9067167744 | bytes 16228352 | tf_op jit(solution)/shard_map/dot_general | solution.py:8
  261.6 0.0 reduce-scatter.5.cloned.1.call-update
  261.6 0.0 reduce-scatter.3.cloned.1.call-start
  261.7 1.3 copy-done.7
  263.0 7.9 fusion.14.clone.5
  271.0 12.8 %convolution_convert_fusion.1 = bf16[2048,2880]{1,0:T(8,128)(2,1)} fusion(s32[2048]{0:T(1024)S(1)} %fusion.30, bf16[768,2880]{0,1:T(8,128)(2,1)S(1)} %fusion.14.clone.5), kind=kOutput, calls=%fused_computation.1 | convolution fusion | flops 9067167744 | bytes 16228352 | tf_op jit(solution)/shard_map/dot_general | solution.py:8
  283.8 0.0 reduce-scatter.3.cloned.1.call-update
  283.8 5.2 all-to-all-start
  288.9 0.0 copy-start.6
  289.0 0.0 slice-start.2
  289.0 9.0 %convert_bitcast_fusion = bf16[1,1024,2880]{1,2,0:T(8,128)(2,1)} fusion(bf16[768,2880]{0,1:T(8,128)(2,1)} %copy-done.12, bf16[768,1024]{1,0:T(8,128)(2,1)S(1)} %copy-done.7), kind=kOutput, calls=%fused_computation.21 | convolution fusion | flops 4532797440 | bytes 11894784 | tf_op jit(solution)/shard_map/dot_general | solution.py:8
  298.0 0.0 copy-done.6
  298.0 9.0 %convert_bitcast_fusion.1 = bf16[1,2880,1024]{2,1,0:T(8,128)(2,1)} fusion(bf16[768,2880]{0,1:T(8,128)(2,1)} %copy-done.11, bf16[768,1024]{1,0:T(8,128)(2,1)S(1)} %copy-done.6), kind=kOutput, calls=%fused_computation.22 | convolution fusion | flops 4532797440 | bytes 11894784 | tf_op jit(solution)/shard_map/dot_general | solution.py:8
  307.0 0.0 slice-done.3
  307.0 0.0 copy-start.9
  307.0 0.0 copy-start.1
  307.0 6.6 convert_bitcast_fusion.2
  313.6 0.0 all-to-all-done
  313.7 6.0 psum.7
  319.6 200.6 %reduce-scatter.5.cloned.1.call-done = bf16[64,2880]{1,0:T(8,128)(2,1)} async-done(((bf16[2048,2880]{1,0:T(8,128)(2,1)}), bf16[64,2880]{1,0:T(8,128)(2,1)}) %reduce-scatter.5.cloned.1.call-update) | async-done | bytes 368656 | tf_op jit(solution)/shard_map/reduce_scatter | solution.py:64
  520.2 10.6 %all_gather.19 = bf16[128,2880]{1,0:T(8,128)(2,1)S(1)} all-gather(bf16[64,2880]{1,0:T(8,128)(2,1)} %reduce-scatter.5.cloned.1.call-done), channel_id=1, replica_groups=mesh['seq'=16,'exp'=2] {'exp'}, dimensions={0}, use_global_device_ids=true | all-gather | bytes 1105920 | tf_op jit(solution)/shard_map/all_gather | solution.py:75
  530.9 1.1 copy.31
  532.0 251.5 %reduce-scatter.3.cloned.1.call-done = bf16[64,2880]{1,0:T(8,128)(2,1)} async-done(((bf16[2048,2880]{1,0:T(8,128)(2,1)}), bf16[64,2880]{1,0:T(8,128)(2,1)}) %reduce-scatter.3.cloned.1.call-update) | async-done | bytes 368656 | tf_op jit(solution)/shard_map/reduce_scatter | solution.py:54
  783.5 10.8 %all_gather.17 = bf16[128,2880]{1,0:T(8,128)(2,1)S(1)} all-gather(bf16[64,2880]{1,0:T(8,128)(2,1)} %reduce-scatter.3.cloned.1.call-done), channel_id=1, replica_groups=mesh['seq'=16,'exp'=2] {'exp'}, dimensions={0}, use_global_device_ids=true | all-gather | bytes 1105920 | tf_op jit(solution)/shard_map/all_gather | solution.py:75
  794.3 1.1 copy.30
  (19 shorter events, 0.1 us)
Async XLA Ops:
  7.2 1.1 copy-start
  7.2 4.9 copy-start.8
  7.2 4.9 copy-start.10
  7.2 98.7 %all-gather.3.cloned.1.call-start = ((), (), s32[]{:S(2)}) async-start(), calls=%async_computation.3 | async-start | bytes 12435456 | tf_op jit(solution)/shard_map/all_gather | solution.py:23
  9.6 191.8 %all-gather.5.cloned.1.call-start = ((), (), s32[]{:S(2)}) async-start(), calls=%async_computation.5 | async-start | bytes 12435456 | tf_op jit(solution)/shard_map/all_gather | solution.py:26
  12.1 508.2 %reduce-scatter.5.cloned.1.call-start = ((), (), s32[]{:S(2)}) async-start(), calls=%async_computation.6 | async-start | bytes 12435456 | tf_op jit(solution)/shard_map/reduce_scatter | solution.py:64
  119.2 8.8 %copy-start.11 = (bf16[768,2880]{0,1:T(8,128)(2,1)}, bf16[768,2880]{0,1:T(8,128)(2,1)S(1)}, u32[]{:S(2)}) copy-start(bf16[768,2880]{0,1:T(8,128)(2,1)S(1)} %fusion.17) | copy-start | bytes 13271044
  201.4 13.6 %copy-start.2 = (f32[768,1024]{1,0:T(8,128)S(1)}, f32[768,1024]{1,0:T(8,128)}, u32[]{:S(2)}) copy-start(f32[768,1024]{1,0:T(8,128)} %fusion.8) | copy-start | bytes 9437188
  215.1 9.4 %copy-start.12 = (bf16[768,2880]{0,1:T(8,128)(2,1)}, bf16[768,2880]{0,1:T(8,128)(2,1)S(1)}, u32[]{:S(2)}) copy-start(bf16[768,2880]{0,1:T(8,128)(2,1)S(1)} %fusion.18) | copy-start | bytes 13271044
  226.7 14.7 %slice-start = ((s8[5898240]{0:T(1024)(128)(4,1)}), s8[4194304]{0:T(1024)(128)(4,1)S(1)}, s32[]{:S(2)}) async-start(s8[5898240]{0:T(1024)(128)(4,1)} %bitcast.66), calls=%async_computation.7 | async-start | bytes 8388608
  230.3 11.2 %copy-start.5 = (bf16[768,1024]{1,0:T(8,128)(2,1)}, bf16[768,1024]{1,0:T(8,128)(2,1)S(1)}, u32[]{:S(2)}) copy-start(bf16[768,1024]{1,0:T(8,128)(2,1)S(1)} %get-tuple-element.35) | copy-start | bytes 4718596
  230.3 11.2 %copy-start.3 = (bf16[768,1024]{1,0:T(8,128)(2,1)}, bf16[768,1024]{1,0:T(8,128)(2,1)S(1)}, u32[]{:S(2)}) copy-start(bf16[768,1024]{1,0:T(8,128)(2,1)S(1)} %get-tuple-element.34) | copy-start | bytes 4718596
  230.3 11.2 %slice-start.1 = ((s8[5898240]{0:T(1024)(128)(4,1)}), s8[1703936]{0:T(1024)(128)(4,1)S(1)}, s32[]{:S(2)}) async-start(s8[5898240]{0:T(1024)(128)(4,1)} %bitcast.66), calls=%async_computation.8 | async-start | bytes 3407872
  261.6 1.4 copy-start.7
  261.6 521.8 %reduce-scatter.3.cloned.1.call-start = ((), (), s32[]{:S(2)}) async-start(), calls=%async_computation.4 | async-start | bytes 12435456 | tf_op jit(solution)/shard_map/reduce_scatter | solution.py:54
  283.8 29.9 %all-to-all-start = ((f32[16,1,128]{2,1,0:T(1,128)}), f32[16,1,128]{2,1,0:T(1,128)S(1)}, u32[]{:S(2)}, u32[]{:S(2)}) async-start(f32[16,1,128]{2,1,0:T(1,128)} %bitcast.6), calls=%async_computation.2 | async-start | bytes 16384 | tf_op jit(solution)/shard_map/all_to_all | solution.py:67
  288.9 9.0 %copy-start.6 = (bf16[768,1024]{1,0:T(8,128)(2,1)S(1)}, bf16[768,1024]{1,0:T(8,128)(2,1)}, u32[]{:S(2)}) copy-start(bf16[768,1024]{1,0:T(8,128)(2,1)} %copy-done.5) | copy-start | bytes 4718596
  289.0 18.0 %slice-start.2 = ((s8[4423680]{0:T(1024)(128)(4,1)}), s8[4194304]{0:T(1024)(128)(4,1)S(1)}, s32[]{:S(2)}) async-start(s8[4423680]{0:T(1024)(128)(4,1)} %bitcast.68), calls=%async_computation.9 | async-start | bytes 8388608
  298.0 9.0 %copy-start.4 = (bf16[768,1024]{1,0:T(8,128)(2,1)S(1)}, bf16[768,1024]{1,0:T(8,128)(2,1)}, u32[]{:S(2)}) copy-start(bf16[768,1024]{1,0:T(8,128)(2,1)} %copy-done.3) | copy-start | bytes 4718596
  298.0 9.0 %slice-start.3 = ((s8[4423680]{0:T(1024)(128)(4,1)}), s8[229376]{0:T(1024)(128)(4,1)S(1)}, s32[]{:S(2)}) async-start(s8[4423680]{0:T(1024)(128)(4,1)} %bitcast.68), calls=%async_computation.10 | async-start | bytes 458752
  307.0 6.7 copy-start.9
  307.0 488.5 %copy-start.1 = (bf16[128,2880]{0,1:T(8,128)(2,1)S(1)}, bf16[128,2880]{0,1:T(8,128)(2,1)}, u32[]{:S(2)}) copy-start(bf16[128,2880]{0,1:T(8,128)(2,1)} %param.7) | copy-start | bytes 2211844
Sparse Core Ops, SparseCore 0:
  11.5 94.3 all-gather.2
  109.4 91.9 all-gather.4
  261.8 258.4 reduce-scatter.4
  522.5 260.9 reduce-scatter.2

commit v2 on v1

v2 whole, which is shorter than its diff:
```python
import functools

import jax
import jax.numpy as jnp
from jax import lax
from jax.experimental import pallas as pl
from jax.experimental.pallas import tpu as pltpu
from jax.sharding import PartitionSpec as P

MESH = pl.DeviceIdType.MESH


def dot(left, right, dims):
    return lax.dot_general(left, right, (dims, ((), ())), preferred_element_type=jnp.float32)


def greet(n, m, me, mine):
    barrier = pltpu.get_barrier_semaphore()

    @pl.loop(1, n)
    def _(j):
        pl.semaphore_signal(
            barrier, inc=1, device_id=(lax.rem(me + j, n), mine), device_id_type=MESH
        )

    for q in range(1, m):
        pl.semaphore_signal(
            barrier, inc=1, device_id=(me, lax.rem(mine + q, m)), device_id_type=MESH
        )
    pl.semaphore_wait(barrier, n + m - 2)


def dispatch_kernel(n, m, x_in, r_in, x_out, r_out, send, recv, fsend, frecv, own):
    me = lax.axis_index("seq")
    mine = lax.axis_index("exp")
    per = n // m
    arrays = ((x_in, x_out), (r_in, r_out))
    out_first = lax.rem(mine + m * n - 2 * me, m)

    def in_first(plane):
        return lax.rem(2 * me + m - plane, m)

    def across(a, i, block, place, target):
        src, dst = arrays[a]
        return pltpu.make_async_remote_copy(
            src_ref=src.at[block],
            dst_ref=dst.at[place],
            send_sem=send.at[a, i],
            recv_sem=recv.at[a, i],
            device_id=(target, mine),
            device_id_type=MESH,
        )

    def onward(a, i, q, block):
        dst = arrays[a][1]
        return pltpu.make_async_remote_copy(
            src_ref=dst.at[block],
            dst_ref=dst.at[block],
            send_sem=fsend.at[a, i, q - 1],
            recv_sem=frecv.at[a, i, q - 1],
            device_id=(me, lax.rem(mine + q, m)),
            device_id_type=MESH,
        )

    greet(n, m, me, mine)
    for a in range(2):
        pltpu.make_async_copy(arrays[a][0].at[me], arrays[a][1].at[me], own.at[a]).start()

    for a in range(2):

        @pl.loop(0, per)
        def _(i):
            j = m * i + out_first
            target = lax.rem(me + j, n)

            @pl.when(j > 0)
            def _():
                across(a, i, target, me, target).start()

    for a in range(2):

        @pl.loop(0, per)
        def _(i):
            j = m * i + in_first(mine)
            source = lax.rem(me + n - j, n)

            @pl.when(j > 0)
            def _():
                across(a, i, source, source, source).wait_recv()
                for q in range(1, m):
                    onward(a, i, q, source).start()

    for a in range(2):

        @pl.loop(0, per)
        def _(i):
            j = m * i + out_first
            target = lax.rem(me + j, n)

            @pl.when(j > 0)
            def _():
                across(a, i, target, me, target).wait_send()

            k = m * i + in_first(mine)
            for q in range(1, m):

                @pl.when(k > 0)
                def _(q=q):
                    onward(a, i, q, lax.rem(me + n - k, n)).wait_send()

                h = m * i + in_first(lax.rem(mine + m - q, m))

                @pl.when(h > 0)
                def _(q=q, h=h):
                    onward(a, i, q, lax.rem(me + n - h, n)).wait_recv()

        pltpu.make_async_copy(arrays[a][0].at[me], arrays[a][1].at[me], own.at[a]).wait()


def dispatch(n, m, x_send, r_send):
    shape = jax.ShapeDtypeStruct(x_send.shape, x_send.dtype)
    per = n // m
    sent = x_send.size * 2
    return pl.pallas_call(
        functools.partial(dispatch_kernel, n, m),
        out_shape=(shape, shape),
        in_specs=[pl.BlockSpec(memory_space=pl.ANY)] * 2,
        out_specs=[pl.BlockSpec(memory_space=pl.ANY)] * 2,
        scratch_shapes=[
            pltpu.SemaphoreType.DMA((2, per)),
            pltpu.SemaphoreType.DMA((2, per)),
            pltpu.SemaphoreType.DMA((2, per, m - 1)),
            pltpu.SemaphoreType.DMA((2, per, m - 1)),
            pltpu.SemaphoreType.DMA((2,)),
        ],
        compiler_params=pltpu.CompilerParams(collective_id=0, has_side_effects=True),
        cost_estimate=pl.CostEstimate(flops=0, bytes_accessed=4 * sent, transcendentals=0),
    )(x_send, r_send)


def back_kernel(n, m, y_in, dx_in, y_out, dx_out, part, total, psend, precv, send, recv):
    me = lax.axis_index("seq")
    mine = lax.axis_index("exp")
    per = n // m
    arrays = ((y_in, y_out), (dx_in, dx_out))

    def slab(i, plane):
        return m * i + lax.rem(plane + m * n - me, m)

    def over(a, i, q):
        plane = lax.rem(mine + q, m)
        return pltpu.make_async_remote_copy(
            src_ref=arrays[a][0].at[slab(i, plane)],
            dst_ref=part.at[a, q - 1, i],
            send_sem=psend.at[a, q - 1, i],
            recv_sem=precv.at[a, q - 1, i],
            device_id=(me, plane),
            device_id_type=MESH,
        )

    def home(a, i, target, place):
        return pltpu.make_async_remote_copy(
            src_ref=total.at[a, i],
            dst_ref=arrays[a][1].at[place],
            send_sem=send.at[a, i],
            recv_sem=recv.at[a, place],
            device_id=(target, mine),
            device_id_type=MESH,
        )

    greet(n, m, me, mine)
    turn = me // m
    for a in range(2):

        @pl.loop(0, per)
        def _(i):
            for q in range(1, m):
                over(a, lax.rem(i + turn, per), q).start()

    for a in range(2):

        @pl.loop(0, per)
        def _(step):
            i = lax.rem(step + turn, per)
            s = slab(i, mine)
            summed = arrays[a][0][s].astype(jnp.float32)
            for q in range(1, m):
                over(a, i, q).wait_recv()
                summed = summed + part[a, q - 1, i].astype(jnp.float32)
            total[a, i] = summed.astype(jnp.bfloat16)

            @pl.when(s != me)
            def _():
                home(a, i, s, me // m).start()

            @pl.when(s == me)
            def _():
                arrays[a][1][me // m] = total[a, i]

    for a in range(2):

        @pl.loop(0, per)
        def _(i):
            for q in range(1, m):
                over(a, i, q).wait_send()
            s = slab(i, mine)

            @pl.when(s != me)
            def _():
                home(a, i, s, me // m).wait_send()
                home(a, i, s, i).wait_recv()


def back(n, m, y_part, dx_part):
    per = n // m
    block = y_part.shape[1:]
    shape = jax.ShapeDtypeStruct((per, *block), y_part.dtype)
    sent = y_part.size * 2
    return pl.pallas_call(
        functools.partial(back_kernel, n, m),
        out_shape=(shape, shape),
        in_specs=[pl.BlockSpec(memory_space=pltpu.VMEM)] * 2,
        out_specs=[pl.BlockSpec(memory_space=pltpu.VMEM)] * 2,
        scratch_shapes=[
            pltpu.VMEM((2, m - 1, per, *block), jnp.bfloat16),
            pltpu.VMEM((2, per, *block), jnp.bfloat16),
            pltpu.SemaphoreType.DMA((2, m - 1, per)),
            pltpu.SemaphoreType.DMA((2, m - 1, per)),
            pltpu.SemaphoreType.DMA((2, per)),
            pltpu.SemaphoreType.DMA((2, per)),
        ],
        compiler_params=pltpu.CompilerParams(
            collective_id=1, has_side_effects=True, vmem_limit_bytes=48 * 2**20
        ),
        cost_estimate=pl.CostEstimate(flops=0, bytes_accessed=4 * sent, transcendentals=0),
    )(y_part, dx_part)


def body(tokens, expert_ids, route_weights, cotangent, w_gate, w_up, w_down):
    tok, width = tokens.shape
    top = expert_ids.shape[1]
    n = lax.axis_size("seq")
    m = lax.axis_size("exp")
    capacity = 3 * tok * top // (2 * n)
    total = n * capacity
    me = lax.axis_index("seq")
    mine = lax.axis_index("exp")

    named = expert_ids[:, :, None] == jnp.arange(n, dtype=jnp.int32)[None, None, :]
    hits = jnp.any(named, axis=1)
    earlier = (jnp.arange(tok)[:, None] > jnp.arange(tok)[None, :]).astype(jnp.bfloat16)
    before = dot(earlier, hits.astype(jnp.bfloat16), ((1,), (0,))).astype(jnp.int32)
    slot = jnp.sum(jnp.where(named, before[:, None, :], 0), axis=2)
    target = expert_ids * capacity + slot
    rows = jnp.arange(total, dtype=jnp.int32)
    here = target.T[:, None, :] == rows[None, :, None]
    pick = jnp.any(here, axis=0).astype(jnp.bfloat16)
    g_row = jnp.sum(jnp.where(here, route_weights.T[:, None, :], 0.0), axis=(0, 2))
    x_send = dot(pick, tokens, ((1,), (0,))).astype(jnp.bfloat16)
    r_send = (dot(pick, cotangent, ((1,), (0,))) * g_row[:, None]).astype(jnp.bfloat16)
    blocks = (n, capacity, width)
    x_rows, r_rows = dispatch(n, m, x_send.reshape(blocks), r_send.reshape(blocks))
    x_rows = x_rows.reshape(total, width)
    r_rows = r_rows.reshape(total, width)

    wg, wu, wd = w_gate[0], w_up[0], w_down[0]
    gate = dot(x_rows, wg, ((1,), (0,)))
    up = dot(x_rows, wu, ((1,), (0,)))
    sigma = jax.nn.sigmoid(gate)
    silu = gate * sigma
    hidden_f = silu * up
    hidden = hidden_f.astype(jnp.bfloat16)
    y_part = dot(hidden, wd, ((1,), (0,))).astype(jnp.bfloat16)
    d_hidden = dot(r_rows, wd, ((1,), (1,)))
    d_gate = (d_hidden * up * sigma * (1.0 + gate * (1.0 - sigma))).astype(jnp.bfloat16)
    d_up = (d_hidden * silu).astype(jnp.bfloat16)
    wgt = jnp.sum(hidden_f * d_hidden, axis=1)
    dx_part = (dot(d_gate, wg, ((1,), (1,))) + dot(d_up, wu, ((1,), (1,)))).astype(jnp.bfloat16)
    y_back, dx_back = back(n, m, y_part.reshape(blocks), dx_part.reshape(blocks))

    wgt_back = lax.all_to_all(
        wgt.reshape(n, capacity), "seq", split_axis=0, concat_axis=0, tiled=True
    ).reshape(total)
    route = target[:, :, None] == rows[None, None, :]
    products = jnp.sum(jnp.where(route, wgt_back[None, None, :], 0.0), axis=2) / route_weights

    kept = total // m
    place = jnp.arange(kept, dtype=jnp.int32)
    kept_expert = place // capacity * m + lax.rem(mine + m * n - me, m)
    kept_row = kept_expert * capacity + lax.rem(place, capacity)
    kept_route = target[:, :, None] == kept_row[None, None, :]
    weight = jnp.sum(jnp.where(kept_route, route_weights[:, :, None], 0.0), axis=1)
    high = weight.astype(jnp.bfloat16)
    low = (weight - high.astype(jnp.float32)).astype(jnp.bfloat16)
    y_flat = y_back.reshape(kept, width)
    y_sum = dot(high, y_flat, ((1,), (0,))) + dot(low, y_flat, ((1,), (0,)))
    one = jnp.any(kept_route, axis=1).astype(jnp.bfloat16)
    dx_sum = dot(one, dx_back.reshape(kept, width), ((1,), (0,)))
    y_full, dx_full, weight_grad = lax.psum((y_sum, dx_sum, products), "exp")

    g_gate = dot(x_rows, d_gate, ((0,), (0,))).astype(jnp.bfloat16)
    g_up = dot(x_rows, d_up, ((0,), (0,))).astype(jnp.bfloat16)
    g_down = dot(hidden, r_rows, ((0,), (0,))).astype(jnp.bfloat16)
    return (
        y_full.astype(jnp.bfloat16),
        dx_full.astype(jnp.bfloat16),
        weight_grad,
        g_gate[None],
        g_up[None],
        g_down[None],
    )


def solution(mesh):
    rows = P("seq", None)
    columns = P("seq", None, "exp")
    down = P("seq", "exp", None)
    return jax.shard_map(
        body,
        mesh=mesh,
        in_specs=(rows, rows, rows, rows, columns, columns, down),
        out_specs=(rows, rows, rows, columns, columns, down),
        check_vma=False,
    )
```

time: 813 us -> 467 us (0.57); the launches traced: 802 us -> 466 us
  waiting for transfers between devices: 595 us -> 0.01 us
  Pallas kernels: 0 us -> 269 us
  matrix products: 130 us -> 84.8 us
  blocking collectives: 42.8 us -> 74.3 us
  local copies, waits for them, and re-layouts: 8.4 us -> 27.6 us
  between operations: 14.5 us -> 0.99 us
    reduce_scatter x2 -> x0, waiting for transfers between devices: 452 us -> none  [the longest x1 251 us: body(): moe = lax.psum_scatter(y_all, both, scatter_dimension=0, tiled=True)]
    pallas_call x0 -> x2, Pallas kernels: none -> 269 us  [the longest x1 144 us: dispatch(): pl.pallas_call(functools.partial(dispatch_kernel, n, m), out_shape=(shape...]
    all_gather x2 -> x0, waiting for transfers between devices: 143 us -> none  [the longest x1 78 us: body(): lax.all_gather(lax.dynamic_slice_in_dim(tokens, mine * share, share, 0),...]
    psum x1, blocking collectives: 5.97 us -> 74.3 us  [body(): y_full, dx_full, weight_grad = lax.psum((y_sum, dx_sum, products), 'exp')]
    dot_general x14 -> x15, matrix products: 130 us -> 84.8 us  [dot(): lax.dot_general(left, right, (dims, ((), ())), preferred_element_type=jnp...]
    all_gather x3 -> x0, blocking collectives: 36.9 us -> none  [the longest x2 21.5 us: body(): moe, dx = lax.all_gather((moe, dx), 'exp', axis=0, tiled=True)]
    convert_element_type x0 -> x4, local copies, waits for them, and re-layouts: none -> 26.2 us  [the longest x1 6.58 us: body(): (dot(pick, cotangent, ((1,), (0,))) * g_row[:, None]).astype(jnp.bfloat16)]
  transfers between devices with their start and end apart: 5 -> 1, of which waited for: 4 -> 0; matrix products, arithmetic and copies ran while one was open for 10% -> 14% of each run, Pallas kernels for 0% -> 27%
where the time goes in v2:
time: 467 us; the launch traced here: 466 us
  Pallas kernels  269 us (58%)
  matrix products  84.8 us (18%)
  blocking collectives  74.3 us (16%)
  local copies, waits for them, and re-layouts  27.6 us (6%)
  other arithmetic  4.69 us (1%)
    pallas_call x1, Pallas kernels, dispatch(): pl.pallas_call(functools.partial(dispatch_kernel, n, m), out_shape=(shape...  144 us
    pallas_call x1, Pallas kernels, back(): pl.pallas_call(functools.partial(back_kernel, n, m), out_shape=(shape, sh...  125 us
    dot_general x15, matrix products, dot(): lax.dot_general(left, right, (dims, ((), ())), preferred_element_type=jnp...  84.8 us
    psum x1, blocking collectives, body(): y_full, dx_full, weight_grad = lax.psum((y_sum, dx_sum, products), 'exp')  74.3 us
  transfers between devices with their start and end apart: 1, of which 0 were waited for; matrix products, arithmetic and copies ran while one was open for 14% of the time, Pallas kernels for 27%

profile of v2, /device:TPU:12, one launch (start us, length us, event | category | flops | bytes accessed | tf_op | source)
XLA Modules:
  0.0 465.6 jit_solution(10158278577014396905)
XLA Ops:
  0.6 0.0 copy-start
  0.6 0.8 fusion.23
  1.4 0.1 convolution_convert_fusion.1
  1.6 0.7 select_reduce_fusion.2
  2.3 0.7 multiply_add_fusion
  3.0 0.2 fusion.18
  3.2 0.9 select_reduce_fusion.1
  4.1 0.0 copy-done
  4.1 3.4 multiply_convert_fusion
  7.5 6.6 %copy.23 = bf16[768,2880]{1,0:T(8,128)(2,1)} copy(bf16[768,2880]{0,1:T(8,128)(2,1)} %multiply_convert_fusion) | data formatting | bytes 8847360 | tf_op jit(solution)/shard_map/convert_element_type | solution.py:260
  14.1 0.0 copy-done.2
  14.1 3.4 convolution_convert_fusion
  17.5 6.5 %copy.22 = bf16[768,2880]{1,0:T(8,128)(2,1)} copy(bf16[768,2880]{0,1:T(8,128)(2,1)} %convolution_convert_fusion) | data formatting | bytes 8847360 | tf_op jit(solution)/shard_map/convert_element_type | solution.py:259
  24.0 144.2 %shard_map.118 = (bf16[16,48,2880]{2,1,0:T(8,128)(2,1)}, bf16[16,48,2880]{2,1,0:T(8,128)(2,1)}) custom-call(bf16[16,48,2880]{2,1,0:T(8,128)(2,1)} %bitcast.63, bf16[16,48,2880]{2,1,0:T(8,128)(2,1)} %bitcast.61), custom_call_target="tpu_custom_call" | custom-call | bytes 17694720 | tf_op jit(solution)/shard_map/pallas_call | solution.py:124
  168.3 0.0 copy-start.4
  168.3 0.0 slice-start
  168.3 0.0 slice-start.6
  168.3 9.1 %fusion.10 = f32[768,1024]{1,0:T(8,128)S(1)} fusion(bf16[768,2880]{1,0:T(8,128)(2,1)} %bitcast.72, bf16[1,2880,1024]{2,1,0:T(8,128)(2,1)} %param.11), kind=kOutput, calls=%fused_computation.12 | convolution fusion | flops 4529848320 | bytes 13467648 | tf_op jit(solution)/shard_map/dot_general | solution.py:14
  177.4 0.0 copy-done.4
  177.4 0.0 slice-start.1
  177.4 0.0 slice-start.7
  177.4 7.2 %fusion.6 = f32[768,1024]{1,0:T(8,128)S(1)} fusion(bf16[768,2880]{1,0:T(8,128)(2,1)S(1)} %bitcast.73, bf16[1,2880,1024]{2,1,0:T(8,128)(2,1)} %param.12), kind=kOutput, calls=%fused_computation.8 | convolution fusion | flops 4529848320 | bytes 13467648 | tf_op jit(solution)/shard_map/dot_general | solution.py:14
  184.6 0.0 slice-done
  184.6 0.0 slice-done.6
  184.6 0.0 slice-done.1
  184.7 0.0 copy-start.3
  184.7 0.0 slice-start.4
  184.7 7.9 %multiply_reduce_fusion = (f32[768]{0:T(1024)S(1)}, bf16[768,1024]{1,0:T(8,128)(2,1)}, bf16[768,1024]{1,0:T(8,128)(2,1)}, bf16[768,1024]{1,0:T(8,128)(2,1)}) fusion(f32[768,1024]{1,0:T(8,128)S(1)} %fusion.6, f32[768,1024]{1,0:T(8,128)S(1)} %fusion.10, bf16[768,2880]{1,0:T(8,128)(2,1)S(1)} %bitcast.80, bf16[1,1024,2880]{1,2,0:T(8,128)(2,1)S(1)} %bitcast.69), kind=kOutput, calls=%fused_computation.20 | convolution fusion | flops 4543216640 | bytes 21335040 | tf_op jit(solution)/shard_map/dot_general | solution.py:14
  192.6 0.7 all_to_all.6
  193.3 4.2 all-to-all-start
  197.6 0.2 fusion.19
  197.8 0.2 compare_reduce_fusion
  197.9 0.0 slice-start.5
  197.9 0.0 copy-start.7
  197.9 0.0 slice-start.8
  198.0 11.5 %fusion.4 = f32[768,2880]{0,1:T(8,128)} fusion(bf16[768,1024]{1,0:T(8,128)(2,1)} %get-tuple-element.20, bf16[1,2880,1024]{2,1,0:T(8,128)(2,1)} %param.12), kind=kOutput, calls=%fused_computation.6 | convolution fusion | flops 4529848320 | bytes 16318464 | tf_op jit(solution)/shard_map/dot_general | solution.py:14
  209.5 0.0 slice-done.4
  209.5 0.0 copy-done.7
  209.5 0.0 copy-start.5
  209.5 0.0 slice-start.9
  209.5 6.6 %convert_bitcast_fusion.1 = bf16[1,2880,1024]{2,1,0:T(8,128)(2,1)} fusion(bf16[768,2880]{1,0:T(8,128)(2,1)S(1)} %bitcast.76, bf16[768,1024]{1,0:T(8,128)(2,1)S(1)} %copy-done.7), kind=kOutput, calls=%fused_computation.15 | convolution fusion | flops 4532797440 | bytes 11894784 | tf_op jit(solution)/shard_map/dot_general | solution.py:14
  216.1 9.1 %fusion.12 = bf16[768,2880]{0,1:T(8,128)(2,1)} fusion(bf16[768,1024]{1,0:T(8,128)(2,1)S(1)} %copy-done.5, bf16[1,1024,2880]{1,2,0:T(8,128)(2,1)} %param.13), kind=kOutput, calls=%fused_computation.17 | convolution fusion | flops 4532060160 | bytes 11894784 | tf_op jit(solution)/shard_map/dot_general | solution.py:14
  225.3 0.0 slice-done.8
  225.3 0.0 slice-start.10
  225.3 0.0 slice-start.11
  225.3 6.8 %convert_bitcast_fusion = bf16[1,1024,2880]{1,2,0:T(8,128)(2,1)} fusion(bf16[768,1024]{1,0:T(8,128)(2,1)S(1)} %copy-done.5, bf16[768,2880]{1,0:T(8,128)(2,1)S(1)} %bitcast.83), kind=kOutput, calls=%fused_computation.14 | convolution fusion | flops 4532797440 | bytes 11894784 | tf_op jit(solution)/shard_map/dot_general | solution.py:14
  232.1 8.7 %convert_bitcast_fusion.2 = bf16[1,2880,1024]{2,1,0:T(8,128)(2,1)} fusion(bf16[768,2880]{1,0:T(8,128)(2,1)S(1)} %bitcast.77, bf16[768,1024]{1,0:T(8,128)(2,1)} %get-tuple-element.18), kind=kOutput, calls=%fused_computation.16 | convolution fusion | flops 4532797440 | bytes 11894784 | tf_op jit(solution)/shard_map/dot_general | solution.py:14
  240.7 0.0 slice-done.3
  240.8 0.0 slice-done.12
  240.8 0.0 copy-done.6
  240.8 6.8 %add_convert_fusion = bf16[768,2880]{0,1:T(8,128)(2,1)} fusion(f32[768,2880]{0,1:T(8,128)S(1)} %bitcast.85, bf16[768,1024]{1,0:T(8,128)(2,1)S(1)} %copy-done.6, bf16[1,2880,1024]{2,1,0:T(8,128)(2,1)S(1)} %bitcast.71), kind=kOutput, calls=%fused_computation | convolution fusion | flops 4534272000 | bytes 20742144 | tf_op jit(solution)/shard_map/dot_general | solution.py:14
  247.6 6.5 %copy.25 = bf16[768,2880]{1,0:T(8,128)(2,1)} copy(bf16[768,2880]{0,1:T(8,128)(2,1)} %add_convert_fusion) | data formatting | bytes 8847360 | tf_op jit(solution)/shard_map/convert_element_type | solution.py:278
  254.1 6.6 %copy.24 = bf16[768,2880]{1,0:T(8,128)(2,1)} copy(bf16[768,2880]{0,1:T(8,128)(2,1)} %fusion.12) | data formatting | bytes 8847360 | tf_op jit(solution)/shard_map/convert_element_type | solution.py:273
  260.7 124.8 %shard_map.119 = (bf16[8,48,2880]{2,1,0:T(8,128)(2,1)S(1)}, bf16[8,48,2880]{2,1,0:T(8,128)(2,1)S(1)}) custom-call(bf16[16,48,2880]{2,1,0:T(8,128)(2,1)} %bitcast.64, bf16[16,48,2880]{2,1,0:T(8,128)(2,1)} %bitcast.62), custom_call_target="tpu_custom_call" | custom-call | bytes 17694720 | tf_op jit(solution)/shard_map/pallas_call | solution.py:219
  385.5 1.0 fusion.21
  386.5 1.0 convolution_add_fusion
  387.5 0.0 copy-start.1
  387.6 2.2 fusion.31
  389.7 0.0 all-to-all-done
  389.7 0.5 broadcast.57
  390.2 0.7 reduce.3
  390.9 0.1 broadcast_in_dim.79
  391.0 0.3 select_reduce_fusion
  391.3 74.3 %all-reduce.2 = (bf16[128,2880]{0,1:T(8,128)(2,1)}, bf16[128,2880]{0,1:T(8,128)(2,1)}, f32[128,4]{0,1:T(4,128)}) all-reduce(f32[128,2880]{0,1:T(8,128)S(1)} %convolution_add_fusion, f32[128,2880]{0,1:T(8,128)} %fusion.31, f32[128,4]{0,1:T(4,128)S(1)} %div.18), channel_id=1, replica_groups=mesh['seq'=16,'exp'=2] {'exp'}, use_global_device_ids=true, to_apply=%region_5.6 | all-reduce | flops 737792 | bytes 4427776 | tf_op jit(solution)/shard_map/psum | solution.py:299
  (22 shorter events, 0.0 us)
Async XLA Ops:
  0.6 3.5 copy-start
  7.5 6.6 %copy-start.2 = (bf16[128,2880]{0,1:T(8,128)(2,1)S(1)}, bf16[128,2880]{0,1:T(8,128)(2,1)}, u32[]{:S(2)}) copy-start(bf16[128,2880]{0,1:T(8,128)(2,1)} %param.7) | copy-start | bytes 2211844
  168.3 9.1 %copy-start.4 = (bf16[16,48,2880]{2,1,0:T(8,128)(2,1)S(1)}, bf16[16,48,2880]{2,1,0:T(8,128)(2,1)}, u32[]{:S(2)}) copy-start(bf16[16,48,2880]{2,1,0:T(8,128)(2,1)} %get-tuple-element.10) | copy-start | bytes 13271044
  168.3 16.4 %slice-start = ((s8[5898240]{0:T(1024)(128)(4,1)}), s8[4194304]{0:T(1024)(128)(4,1)S(1)}, s32[]{:S(2)}) async-start(s8[5898240]{0:T(1024)(128)(4,1)} %bitcast.68), calls=%async_computation.1 | async-start | bytes 8388608
  168.3 16.3 %slice-start.6 = ((s8[4521984]{0:T(1024)(128)(4,1)}), s8[4194304]{0:T(1024)(128)(4,1)S(1)}, s32[]{:S(2)}) async-start(s8[4521984]{0:T(1024)(128)(4,1)} %bitcast.78), calls=%async_computation.7 | async-start | bytes 8388608
  177.4 7.3 %slice-start.1 = ((s8[5898240]{0:T(1024)(128)(4,1)}), s8[1703936]{0:T(1024)(128)(4,1)S(1)}, s32[]{:S(2)}) async-start(s8[5898240]{0:T(1024)(128)(4,1)} %bitcast.68), calls=%async_computation.2 | async-start | bytes 3407872
  177.4 7.2 %slice-start.7 = ((s8[4521984]{0:T(1024)(128)(4,1)}), s8[327680]{0:T(1024)(128)(4,1)S(1)}, s32[]{:S(2)}) async-start(s8[4521984]{0:T(1024)(128)(4,1)} %bitcast.78), calls=%async_computation.8 | async-start | bytes 655360
  184.7 12.9 %copy-start.3 = (f32[128,4]{0,1:T(4,128)S(1)}, f32[128,4]{0,1:T(4,128)}, u32[]{:S(2)}) copy-start(f32[128,4]{0,1:T(4,128)} %param.9) | copy-start | bytes 6148
  184.7 24.8 %slice-start.4 = ((s8[4521984]{0:T(1024)(128)(4,1)}), s8[327680]{0:T(1024)(128)(4,1)S(1)}, s32[]{:S(2)}) async-start(s8[4521984]{0:T(1024)(128)(4,1)} %bitcast.74), calls=%async_computation.5 | async-start | bytes 655360
  193.3 196.4 %all-to-all-start = ((f32[16,1,48]{2,1,0:T(1,128)}), f32[16,1,48]{2,1,0:T(1,128)S(1)}, u32[]{:S(2)}, u32[]{:S(2)}) async-start(f32[16,1,48]{2,1,0:T(1,128)} %all_to_all.6), calls=%async_computation | async-start | bytes 16384 | tf_op jit(solution)/shard_map/all_to_all | solution.py:281
  197.9 11.5 %slice-start.5 = ((s8[4521984]{0:T(1024)(128)(4,1)}), s8[4194304]{0:T(1024)(128)(4,1)S(1)}, s32[]{:S(2)}) async-start(s8[4521984]{0:T(1024)(128)(4,1)} %bitcast.74), calls=%async_computation.6 | async-start | bytes 8388608
  197.9 11.5 %copy-start.7 = (bf16[768,1024]{1,0:T(8,128)(2,1)S(1)}, bf16[768,1024]{1,0:T(8,128)(2,1)}, u32[]{:S(2)}) copy-start(bf16[768,1024]{1,0:T(8,128)(2,1)} %get-tuple-element.20) | copy-start | bytes 4718596
  197.9 27.3 %slice-start.8 = ((s8[4521984]{0:T(1024)(128)(4,1)}), s8[4194304]{0:T(1024)(128)(4,1)S(1)}, s32[]{:S(2)}) async-start(s8[4521984]{0:T(1024)(128)(4,1)} %bitcast.81), calls=%async_computation.9 | async-start | bytes 8388608
  209.5 6.7 %copy-start.5 = (bf16[768,1024]{1,0:T(8,128)(2,1)S(1)}, bf16[768,1024]{1,0:T(8,128)(2,1)}, u32[]{:S(2)}) copy-start(bf16[768,1024]{1,0:T(8,128)(2,1)} %get-tuple-element.19) | copy-start | bytes 4718596
  209.5 15.8 %slice-start.9 = ((s8[4521984]{0:T(1024)(128)(4,1)}), s8[327680]{0:T(1024)(128)(4,1)S(1)}, s32[]{:S(2)}) async-start(s8[4521984]{0:T(1024)(128)(4,1)} %bitcast.81), calls=%async_computation.10 | async-start | bytes 655360
  225.3 15.5 %slice-start.2 = ((s8[5898240]{0:T(1024)(128)(4,1)}), s8[4194304]{0:T(1024)(128)(4,1)S(1)}, s32[]{:S(2)}) async-start(s8[5898240]{0:T(1024)(128)(4,1)} %bitcast.70), calls=%async_computation.3 | async-start | bytes 8388608
  225.3 15.4 %slice-start.10 = ((s8[8847360]{0:T(1024)(128)(4,1)}), s8[458752]{0:T(1024)(128)(4,1)S(1)}, s32[]{:S(2)}) async-start(s8[8847360]{0:T(1024)(128)(4,1)} %bitcast.84), calls=%async_computation.11 | async-start | bytes 917504
  225.3 15.4 %slice-start.11 = ((s8[8847360]{0:T(1024)(128)(4,1)}), s8[4194304]{0:T(1024)(128)(4,1)S(1)}, s32[]{:S(2)}) async-start(s8[8847360]{0:T(1024)(128)(4,1)} %bitcast.84), calls=%async_computation.12 | async-start | bytes 8388608
  232.1 8.7 %slice-start.3 = ((s8[5898240]{0:T(1024)(128)(4,1)}), s8[1703936]{0:T(1024)(128)(4,1)S(1)}, s32[]{:S(2)}) async-start(s8[5898240]{0:T(1024)(128)(4,1)} %bitcast.70), calls=%async_computation.4 | async-start | bytes 3407872
  232.1 8.7 %slice-start.12 = ((s8[8847360]{0:T(1024)(128)(4,1)}), s8[4194304]{0:T(1024)(128)(4,1)S(1)}, s32[]{:S(2)}) async-start(s8[8847360]{0:T(1024)(128)(4,1)} %bitcast.84), calls=%async_computation.13 | async-start | bytes 8388608
  232.1 8.7 %copy-start.6 = (bf16[768,1024]{1,0:T(8,128)(2,1)S(1)}, bf16[768,1024]{1,0:T(8,128)(2,1)}, u32[]{:S(2)}) copy-start(bf16[768,1024]{1,0:T(8,128)(2,1)} %get-tuple-element.18) | copy-start | bytes 4718596
  387.5 78.1 %copy-start.1 = (bf16[128,2880]{0,1:T(8,128)(2,1)S(1)}, bf16[128,2880]{0,1:T(8,128)(2,1)}, u32[]{:S(2)}) copy-start(bf16[128,2880]{0,1:T(8,128)(2,1)} %param.10) | copy-start | bytes 2211844

commit v3 on v2

--- a/solution.py
+++ b/solution.py
@@ -4,6 +4,7 @@
 import jax.numpy as jnp
 from jax import lax
 from jax.experimental import pallas as pl
+from jax.experimental.layout import Layout, with_layout_constraint
 from jax.experimental.pallas import tpu as pltpu
 from jax.sharding import PartitionSpec as P
 
@@ -12,6 +13,10 @@
 
 def dot(left, right, dims):
     return lax.dot_general(left, right, (dims, ((), ())), preferred_element_type=jnp.float32)
+
+
+def row_major(array):
+    return with_layout_constraint(array, Layout(major_to_minor=(0, 1)))
 
 
 def greet(n, m, me, mine):
@@ -258,6 +263,7 @@
     g_row = jnp.sum(jnp.where(here, route_weights.T[:, None, :], 0.0), axis=(0, 2))
     x_send = dot(pick, tokens, ((1,), (0,))).astype(jnp.bfloat16)
     r_send = (dot(pick, cotangent, ((1,), (0,))) * g_row[:, None]).astype(jnp.bfloat16)
+    x_send, r_send = row_major(x_send), row_major(r_send)
     blocks = (n, capacity, width)
     x_rows, r_rows = dispatch(n, m, x_send.reshape(blocks), r_send.reshape(blocks))
     x_rows = x_rows.reshape(total, width)
@@ -276,6 +282,7 @@
     d_up = (d_hidden * silu).astype(jnp.bfloat16)
     wgt = jnp.sum(hidden_f * d_hidden, axis=1)
     dx_part = (dot(d_gate, wg, ((1,), (1,))) + dot(d_up, wu, ((1,), (1,)))).astype(jnp.bfloat16)
+    y_part, dx_part = row_major(y_part), row_major(dx_part)
     y_back, dx_back = back(n, m, y_part.reshape(blocks), dx_part.reshape(blocks))
 
     wgt_back = lax.all_to_all(
@@ -296,8 +303,16 @@
     y_sum = dot(high, y_flat, ((1,), (0,))) + dot(low, y_flat, ((1,), (0,)))
     one = jnp.any(kept_route, axis=1).astype(jnp.bfloat16)
     dx_sum = dot(one, dx_back.reshape(kept, width), ((1,), (0,)))
-    y_full, dx_full, weight_grad = lax.psum((y_sum, dx_sum, products), "exp")
-
+    if m == 2:
+        swap = [(0, 1), (1, 0)]
+        y_own, dx_own = y_sum.astype(jnp.bfloat16), dx_sum.astype(jnp.bfloat16)
+        y_full = y_own.astype(jnp.float32) + lax.ppermute(y_own, "exp", swap).astype(jnp.float32)
+        dx_full = dx_own.astype(jnp.float32) + lax.ppermute(dx_own, "exp", swap).astype(jnp.float32)
+        weight_grad = products + lax.ppermute(products, "exp", swap)
+    else:
+        y_full, dx_full, weight_grad = lax.psum((y_sum, dx_sum, products), "exp")
+
+    d_gate, d_up, hidden, y_back = lax.optimization_barrier((d_gate, d_up, hidden, y_back))
     g_gate = dot(x_rows, d_gate, ((0,), (0,))).astype(jnp.bfloat16)
     g_up = dot(x_rows, d_up, ((0,), (0,))).astype(jnp.bfloat16)
     g_down = dot(hidden, r_rows, ((0,), (0,))).astype(jnp.bfloat16)

time: 467 us -> 378 us (0.81)
  blocking collectives: 74.3 us -> 0 us
  local copies, waits for them, and re-layouts: 27.6 us -> 1.86 us
    psum x1 -> x0, blocking collectives: 74.3 us -> none  [body(): y_full, dx_full, weight_grad = lax.psum((y_sum, dx_sum, products), 'exp')]
    convert_element_type x4 -> x0, local copies, waits for them, and re-layouts: 26.2 us -> none  [the longest x1 6.58 us: body(): (dot(pick, cotangent, ((1,), (0,))) * g_row[:, None]).astype(jnp.bfloat16)]
  transfers between devices with their start and end apart: 1 -> 4, of which waited for: 0 -> 1; matrix products, arithmetic and copies ran while one was open for 14% -> 16% of each run, Pallas kernels for 27% -> 33%
where the time goes in v3:
time: 378 us; the launch traced here: 377 us
  Pallas kernels  269 us (71%)
  matrix products  85.7 us (23%)
  other arithmetic  8.53 us (2%)
  starting transfers between devices  8.35 us (2%)
    pallas_call x1, Pallas kernels, dispatch(): pl.pallas_call(functools.partial(dispatch_kernel, n, m), out_shape=(shape...  144 us
    pallas_call x1, Pallas kernels, back(): pl.pallas_call(functools.partial(back_kernel, n, m), out_shape=(shape, sh...  125 us
    dot_general x15, matrix products, dot(): lax.dot_general(left, right, (dims, ((), ())), preferred_element_type=jnp...  85.7 us
  transfers between devices with their start and end apart: 4, of which 1 were waited for; matrix products, arithmetic and copies ran while one was open for 16% of the time, Pallas kernels for 33%

profile of v3, /device:TPU:12, one launch (start us, length us, event | category | flops | bytes accessed | tf_op | source)
XLA Modules:
  0.0 377.1 jit_solution(3507806313236541946)
XLA Ops:
  0.6 0.0 copy-start
  0.6 0.8 fusion.24
  1.4 0.1 convolution_convert_fusion.2
  1.6 0.7 select_reduce_fusion.2
  2.3 0.7 multiply_add_fusion
  3.0 0.2 fusion.19
  3.2 0.9 select_reduce_fusion.1
  4.1 0.0 copy-done
  4.1 0.0 copy-start.2
  4.1 3.5 convolution_convert_fusion
  7.6 0.0 copy-done.2
  7.6 3.5 multiply_convert_fusion
  11.1 144.2 %shard_map.118 = (bf16[16,48,2880]{2,1,0:T(8,128)(2,1)}, bf16[16,48,2880]{2,1,0:T(8,128)(2,1)}) custom-call(bf16[16,48,2880]{2,1,0:T(8,128)(2,1)} %bitcast.61, bf16[16,48,2880]{2,1,0:T(8,128)(2,1)} %bitcast.62), custom_call_target="tpu_custom_call" | custom-call | bytes 17694720 | tf_op jit(solution)/shard_map/pallas_call | solution.py:129
  155.3 0.0 slice-start.1
  155.3 0.0 copy-start.4
  155.3 0.0 slice-start.2
  155.3 0.0 slice-start.6
  155.3 8.5 %fusion.10 = f32[768,1024]{1,0:T(8,128)S(1)} fusion(bf16[768,2880]{1,0:T(8,128)(2,1)} %bitcast.72, bf16[1,2880,1024]{2,1,0:T(8,128)(2,1)} %param.11), kind=kOutput, calls=%fused_computation.12 | convolution fusion | flops 4529848320 | bytes 13467648 | tf_op jit(solution)/shard_map/dot_general | solution.py:15
  163.9 0.0 slice-done
  163.9 0.0 slice-done.1
  163.9 0.0 copy-done.4
  163.9 0.0 slice-start.3
  163.9 0.0 slice-start.7
  164.0 5.1 %fusion.6 = f32[768,1024]{1,0:T(8,128)S(1)} fusion(bf16[768,2880]{1,0:T(8,128)(2,1)S(1)} %bitcast.74, bf16[1,2880,1024]{2,1,0:T(8,128)(2,1)S(1)} %bitcast.69), kind=kOutput, calls=%fused_computation.8 | convolution fusion | flops 4529848320 | bytes 13467648 | tf_op jit(solution)/shard_map/dot_general | solution.py:15
  169.0 0.0 slice-done.2
  169.1 0.0 slice-done.6
  169.1 0.0 slice-done.3
  169.1 7.7 %multiply_reduce_fusion = (f32[768]{0:T(1024)S(1)}, bf16[768,1024]{1,0:T(8,128)(2,1)S(1)}, bf16[768,1024]{1,0:T(8,128)(2,1)}, bf16[768,1024]{1,0:T(8,128)(2,1)}) fusion(f32[768,1024]{1,0:T(8,128)S(1)} %fusion.6, f32[768,1024]{1,0:T(8,128)S(1)} %fusion.10, bf16[768,2880]{1,0:T(8,128)(2,1)S(1)} %bitcast.80, bf16[1,1024,2880]{1,2,0:T(8,128)(2,1)S(1)} %bitcast.71), kind=kOutput, calls=%fused_computation.22 | convolution fusion | flops 4543216640 | bytes 21335040 | tf_op jit(solution)/shard_map/dot_general | solution.py:15
  176.8 0.8 all_to_all.6
  177.6 4.2 %all-to-all-start = ((f32[16,1,48]{2,1,0:T(1,128)}), f32[16,1,48]{2,1,0:T(1,128)S(1)}, u32[]{:S(2)}, u32[]{:S(2)}) async-start(f32[16,1,48]{2,1,0:T(1,128)} %all_to_all.6), calls=%async_computation | async-start | bytes 16384 | tf_op jit(solution)/shard_map/all_to_all | solution.py:288
  181.8 10.4 %fusion.4 = f32[768,2880]{1,0:T(8,128)} fusion(bf16[768,1024]{1,0:T(8,128)(2,1)} %get-tuple-element.18, bf16[1,2880,1024]{2,1,0:T(8,128)(2,1)} %param.12), kind=kOutput, calls=%fused_computation.6 | convolution fusion | flops 4529848320 | bytes 16318464 | tf_op jit(solution)/shard_map/dot_general | solution.py:15
  192.2 9.4 %fusion.12 = bf16[768,2880]{1,0:T(8,128)(2,1)} fusion(bf16[768,1024]{1,0:T(8,128)(2,1)S(1)} %copy-done.7, bf16[1,1024,2880]{1,2,0:T(8,128)(2,1)} %param.13), kind=kOutput, calls=%fused_computation.17 | convolution fusion | flops 4532060160 | bytes 11894784 | tf_op jit(solution)/shard_map/dot_general | solution.py:15
  201.6 0.2 compare_reduce_fusion
  201.8 0.0 copy-done.5
  201.8 10.8 %add_convert_fusion = bf16[768,2880]{1,0:T(8,128)(2,1)} fusion(f32[768,2880]{1,0:T(8,128)} %fusion.4, bf16[768,1024]{1,0:T(8,128)(2,1)S(1)} %get-tuple-element.17, bf16[1,2880,1024]{2,1,0:T(8,128)(2,1)} %param.11), kind=kOutput, calls=%fused_computation | convolution fusion | flops 4534272000 | bytes 20742144 | tf_op jit(solution)/shard_map/dot_general | solution.py:15
  212.6 124.8 %shard_map.119 = (bf16[8,48,2880]{2,1,0:T(8,128)(2,1)S(1)}, bf16[8,48,2880]{2,1,0:T(8,128)(2,1)S(1)}) custom-call(bf16[16,48,2880]{2,1,0:T(8,128)(2,1)} %bitcast.63, bf16[16,48,2880]{2,1,0:T(8,128)(2,1)} %bitcast.64), custom_call_target="tpu_custom_call" | custom-call | bytes 17694720 | tf_op jit(solution)/shard_map/pallas_call | solution.py:224
  337.4 0.0 slice-start.8
  337.4 1.0 convolution_convert_fusion.1
  338.5 2.1 collective-permute-start.1
  340.6 0.2 fusion.20
  340.8 0.0 slice-start.9
  340.8 0.0 copy-start.8
  340.8 1.0 fusion.22
  341.9 0.0 slice-start.4
  341.9 1.1 fusion.17
  343.0 0.0 slice-start.5
  343.0 0.1 collective-permute-start
  343.1 0.4 copy-done.8
  343.5 6.7 %convert_bitcast_fusion = bf16[1,1024,2880]{1,2,0:T(8,128)(2,1)} fusion(bf16[768,1024]{1,0:T(8,128)(2,1)S(1)} %copy-done.8, bf16[768,2880]{1,0:T(8,128)(2,1)S(1)} %bitcast.83), kind=kOutput, calls=%fused_computation.14 | convolution fusion | flops 4532797440 | bytes 11894784 | tf_op jit(solution)/shard_map/dot_general | solution.py:15
  350.2 0.0 slice-done.5
  350.2 6.6 %convert_bitcast_fusion.1 = bf16[1,2880,1024]{2,1,0:T(8,128)(2,1)} fusion(bf16[768,2880]{1,0:T(8,128)(2,1)S(1)} %bitcast.77, bf16[768,1024]{1,0:T(8,128)(2,1)S(1)} %copy-done.6), kind=kOutput, calls=%fused_computation.15 | convolution fusion | flops 4532797440 | bytes 11894784 | tf_op jit(solution)/shard_map/dot_general | solution.py:15
  356.9 0.0 all-to-all-done
  356.9 0.5 broadcast.57
  357.4 0.7 reduce.3
  358.0 0.1 broadcast_in_dim.79
  358.1 0.3 select_reduce_fusion
  358.5 1.9 collective-permute-start.2
  360.4 10.2 %convert_bitcast_fusion.2 = bf16[1,2880,1024]{2,1,0:T(8,128)(2,1)} fusion(bf16[768,2880]{1,0:T(8,128)(2,1)} %bitcast.73, bf16[768,1024]{1,0:T(8,128)(2,1)} %copy-done.5), kind=kOutput, calls=%fused_computation.16 | convolution fusion | flops 4532797440 | bytes 11894784 | tf_op jit(solution)/shard_map/dot_general | solution.py:15
  370.6 2.7 collective-permute-done.2
  373.3 0.6 add.60
  373.9 0.0 collective-permute-done.1
  373.9 1.1 add_convert_fusion.1
  374.9 0.0 collective-permute-done
  374.9 2.2 add_convert_fusion.2
  (21 shorter events, 0.0 us)
Async XLA Ops:
  0.6 3.5 copy-start
  4.1 3.5 copy-start.2
  11.1 152.8 %slice-start = ((s8[5898240]{0:T(1024)(128)(4,1)}), s8[1703936]{0:T(1024)(128)(4,1)S(1)}, s32[]{:S(2)}) async-start(s8[5898240]{0:T(1024)(128)(4,1)} %bitcast.68), calls=%async_computation.1 | async-start | bytes 3407872
  155.3 8.6 %slice-start.1 = ((s8[5898240]{0:T(1024)(128)(4,1)}), s8[4194304]{0:T(1024)(128)(4,1)S(1)}, s32[]{:S(2)}) async-start(s8[5898240]{0:T(1024)(128)(4,1)} %bitcast.68), calls=%async_computation.2 | async-start | bytes 8388608
  155.3 8.6 %copy-start.4 = (bf16[16,48,2880]{2,1,0:T(8,128)(2,1)S(1)}, bf16[16,48,2880]{2,1,0:T(8,128)(2,1)}, u32[]{:S(2)}) copy-start(bf16[16,48,2880]{2,1,0:T(8,128)(2,1)} %get-tuple-element.13) | copy-start | bytes 13271044
  155.3 13.7 %slice-start.2 = ((s8[5898240]{0:T(1024)(128)(4,1)}), s8[4194304]{0:T(1024)(128)(4,1)S(1)}, s32[]{:S(2)}) async-start(s8[5898240]{0:T(1024)(128)(4,1)} %bitcast.70), calls=%async_computation.3 | async-start | bytes 8388608
  155.3 13.7 %slice-start.6 = ((s8[4521984]{0:T(1024)(128)(4,1)}), s8[4194304]{0:T(1024)(128)(4,1)S(1)}, s32[]{:S(2)}) async-start(s8[4521984]{0:T(1024)(128)(4,1)} %bitcast.78), calls=%async_computation.7 | async-start | bytes 8388608
  163.9 5.1 %slice-start.3 = ((s8[5898240]{0:T(1024)(128)(4,1)}), s8[1703936]{0:T(1024)(128)(4,1)S(1)}, s32[]{:S(2)}) async-start(s8[5898240]{0:T(1024)(128)(4,1)} %bitcast.70), calls=%async_computation.4 | async-start | bytes 3407872
  163.9 5.1 %slice-start.7 = ((s8[4521984]{0:T(1024)(128)(4,1)}), s8[327680]{0:T(1024)(128)(4,1)S(1)}, s32[]{:S(2)}) async-start(s8[4521984]{0:T(1024)(128)(4,1)} %bitcast.78), calls=%async_computation.8 | async-start | bytes 655360
  176.8 25.1 %copy-start.5 = (bf16[768,1024]{1,0:T(8,128)(2,1)}, bf16[768,1024]{1,0:T(8,128)(2,1)S(1)}, u32[]{:S(2)}) copy-start(bf16[768,1024]{1,0:T(8,128)(2,1)S(1)} %get-tuple-element.17) | copy-start | bytes 4718596
  177.6 179.3 %all-to-all-start = ((f32[16,1,48]{2,1,0:T(1,128)}), f32[16,1,48]{2,1,0:T(1,128)S(1)}, u32[]{:S(2)}, u32[]{:S(2)}) async-start(f32[16,1,48]{2,1,0:T(1,128)} %all_to_all.6), calls=%async_computation | async-start | bytes 16384 | tf_op jit(solution)/shard_map/all_to_all | solution.py:288
  181.8 10.4 %copy-start.7 = (bf16[768,1024]{1,0:T(8,128)(2,1)S(1)}, bf16[768,1024]{1,0:T(8,128)(2,1)}, u32[]{:S(2)}) copy-start(bf16[768,1024]{1,0:T(8,128)(2,1)} %get-tuple-element.19) | copy-start | bytes 4718596
  212.6 128.0 %copy-start.3 = (f32[128,4]{0,1:T(4,128)S(1)}, f32[128,4]{0,1:T(4,128)}, u32[]{:S(2)}) copy-start(f32[128,4]{0,1:T(4,128)} %param.9) | copy-start | bytes 6148
  337.4 5.7 %slice-start.8 = ((s8[4521984]{0:T(1024)(128)(4,1)}), s8[327680]{0:T(1024)(128)(4,1)S(1)}, s32[]{:S(2)}) async-start(s8[4521984]{0:T(1024)(128)(4,1)} %bitcast.81), calls=%async_computation.9 | async-start | bytes 655360
  338.5 35.4 %collective-permute-start.1 = (bf16[128,2880]{0,1:T(8,128)(2,1)S(1)}, bf16[128,2880]{0,1:T(8,128)(2,1)S(1)}, u32[]{:S(2)}, u32[]{:S(2)}) collective-permute-start(bf16[128,2880]{0,1:T(8,128)(2,1)S(1)} %convolution_convert_fusion.1), channel_id=1, source_target_pairs={{0,1},{1,0},{2,3},{3,2},{4,5},{5,4},{6,7},{7,6},{8,9},{9,8},{10,11... | collective-permute-start | bytes 2211848 | tf_op jit(solution)/shard_map/ppermute | solution.py:310
  340.8 2.3 slice-start.9
  340.8 2.7 copy-start.8
  341.9 8.3 %slice-start.4 = ((s8[4521984]{0:T(1024)(128)(4,1)}), s8[4194304]{0:T(1024)(128)(4,1)S(1)}, s32[]{:S(2)}) async-start(s8[4521984]{0:T(1024)(128)(4,1)} %bitcast.75), calls=%async_computation.5 | async-start | bytes 8388608
  343.0 7.2 %slice-start.5 = ((s8[4521984]{0:T(1024)(128)(4,1)}), s8[327680]{0:T(1024)(128)(4,1)S(1)}, s32[]{:S(2)}) async-start(s8[4521984]{0:T(1024)(128)(4,1)} %bitcast.75), calls=%async_computation.6 | async-start | bytes 655360
  343.0 7.2 %copy-start.6 = (bf16[768,1024]{1,0:T(8,128)(2,1)S(1)}, bf16[768,1024]{1,0:T(8,128)(2,1)}, u32[]{:S(2)}) copy-start(bf16[768,1024]{1,0:T(8,128)(2,1)} %get-tuple-element.18) | copy-start | bytes 4718596
  343.0 31.9 %collective-permute-start = (bf16[128,2880]{0,1:T(8,128)(2,1)S(1)}, bf16[128,2880]{0,1:T(8,128)(2,1)}, u32[]{:S(2)}, u32[]{:S(2)}) collective-permute-start(bf16[128,2880]{0,1:T(8,128)(2,1)S(1)} %fusion.17), channel_id=1, source_target_pairs={{0,1},{1,0},{2,3},{3,2},{4,5},{5,4},{6,7},{7,6},{8,9},{9,8},{10,11... | collective-permute-start | bytes 2211848 | tf_op jit(solution)/shard_map/ppermute | solution.py:309
  358.5 14.8 %collective-permute-start.2 = (f32[128,4]{0,1:T(4,128)S(1)}, f32[128,4]{0,1:T(4,128)S(1)}, u32[]{:S(2)}, u32[]{:S(2)}) collective-permute-start(f32[128,4]{0,1:T(4,128)S(1)} %div.18), channel_id=1, source_target_pairs={{0,1},{1,0},{2,3},{3,2},{4,5},{5,4},{6,7},{7,6},{8,9},{9,8},{10,11... | collective-permute-start | bytes 6152 | tf_op jit(solution)/shard_map/ppermute | solution.py:311
  360.4 16.7 %copy-start.1 = (bf16[128,2880]{0,1:T(8,128)(2,1)S(1)}, bf16[128,2880]{0,1:T(8,128)(2,1)}, u32[]{:S(2)}) copy-start(bf16[128,2880]{0,1:T(8,128)(2,1)} %param.7) | copy-start | bytes 2211844
